TPU v7x, 32 devices: a whole 2x2x4 slice. The times are simulated.
32 devices in a mesh: fsdp: 4 (over y, x), ctx: 8 (over z, core).
Axes of the slice: x: 2, y: 2, z: 4, core: 2. Of those that a mesh axis runs over, the one named last changes fastest.
Arguments:
- inputs: bfloat16 [4, 2048, 768], P('fsdp', 'ctx'), may hold values from -6 to 6
- positions: int32 [4, 2048], P('fsdp', 'ctx'), may hold values from 0 to 2047, as said below
- in_weight: bfloat16 [768, 2304], P('fsdp'), may hold values from -0.21875 to 0.21875
- in_bias: bfloat16 [2304], P('fsdp'), may hold values from -0.3125 to 0.3125
- out_weight: bfloat16 [768, 768], P('fsdp'), may hold values from -0.109375 to 0.109375
- out_bias: bfloat16 [768], P('fsdp'), may hold values from -4 to 4
- up_weight: bfloat16 [768, 3072], P('fsdp'), may hold values from -0.21875 to 0.21875
- up_bias: bfloat16 [3072], P('fsdp'), may hold values from -6 to 6
- down_weight: bfloat16 [3072, 768], P('fsdp'), may hold values from -0.109375 to 0.109375
- down_bias: bfloat16 [768], P('fsdp'), may hold values from -4 to 4
- first_gain: bfloat16 [768], P('fsdp'), may hold values from 0.25 to 1.75
- first_shift: bfloat16 [768], P('fsdp'), may hold values from -4 to 4
- second_gain: bfloat16 [768], P('fsdp'), may hold values from 0.25 to 1.75
- second_shift: bfloat16 [768], P('fsdp'), may hold values from -4 to 4
- out_grad: bfloat16 [4, 2048, 768], P('fsdp', 'ctx'), may hold values from -6 to 6
Outputs:
- output: bfloat16 [4, 2048, 768], P('fsdp', 'ctx')
- input_gradient: float32 [4, 2048, 768], P('fsdp', 'ctx')
- in_weight_gradient: float32 [768, 2304], P('fsdp')
- in_bias_gradient: float32 [2304], P('fsdp')
- out_weight_gradient: float32 [768, 768], P('fsdp')
- out_bias_gradient: float32 [768], P('fsdp')
- up_weight_gradient: float32 [768, 3072], P('fsdp')
- up_bias_gradient: float32 [3072], P('fsdp')
- down_weight_gradient: float32 [3072, 768], P('fsdp')
- down_bias_gradient: float32 [768], P('fsdp')
- first_gain_gradient: float32 [768], P('fsdp')
- first_shift_gradient: float32 [768], P('fsdp')
- second_gain_gradient: float32 [768], P('fsdp')
- second_shift_gradient: float32 [768], P('fsdp')
Inputs may be any that keep to these rules, and one draw needn't show every extreme that they name: Each row holds every position of its sequence once, in runs of 128 consecutive rising positions that start at multiples of 128; the order of the runs differs from row to row.
All inputs are finite; a program needn't handle non-finite values.
Results may differ from a plain program's by a relative error of at most 0.018.
Values may be sent and summed in bfloat16 or wider, within the bound.
No kernel may reach another device: no remote copies, remote signals or barrier semaphores. Data moves between devices by JAX's collectives and lax.ppermute only.
A program may use at most 192 MiB of HBM per device.

v0:
```python
import math
import jax
import jax.numpy as jnp
from jax import lax
from jax.sharding import PartitionSpec as P

HEAD = 64
ROT = 16
NEG = -1e30
EPS = 1e-05


def from_behind(x, axis, by):
    size = lax.axis_size(axis)
    return lax.ppermute(x, axis, [(i, (i + by) % size) for i in range(size)])


def layer_norm(values, gain, shift):
    mean = jnp.mean(values, -1, keepdims=True)
    centred = values - mean
    spread = jnp.mean(centred * centred, -1, keepdims=True)
    return centred * lax.rsqrt(spread + EPS) * gain + shift


def turn_tables(positions):
    ladder = 10000.0 ** (-jnp.arange(0, ROT, 2, dtype=jnp.float32) / ROT)
    angle = positions.astype(jnp.float32)[..., None] * ladder
    angle = jnp.concatenate([angle, angle], -1)
    return (jnp.cos(angle), jnp.sin(angle))


def rotate(values, cosine, sine):
    half = ROT // 2
    part = values[..., :ROT]
    turned = jnp.concatenate([-part[..., half:], part[..., :half]], -1)
    part = part * cosine[..., None, :] + turned * sine[..., None, :]
    return jnp.concatenate([part, values[..., ROT:]], -1)


def across(left, right):
    return lax.dot_general(
        left, right, (((0,), (0,)), ((), ())), preferred_element_type=jnp.float32
    )


def against(left, right):
    return lax.dot_general(
        left, right, (((1,), (1,)), ((), ())), preferred_element_type=jnp.float32
    )


def softmax_step(carry, queries, query_pos, keys, values, key_pos, scale):
    peak, total, summed = carry
    scores = jnp.einsum("qhd,khd->hqk", queries, keys, preferred_element_type=jnp.float32) * scale
    allowed = (key_pos[None, :] <= query_pos[:, None])[None]
    new_peak = jnp.maximum(peak, jnp.max(jnp.where(allowed, scores, NEG), -1))
    weights = jnp.where(allowed, jnp.exp(scores - new_peak[..., None]), 0.0)
    fade = jnp.exp(peak - new_peak)
    total = total * fade + jnp.sum(weights, -1)
    added = jnp.einsum(
        "hqk,khd->qhd", weights.astype(jnp.bfloat16), values, preferred_element_type=jnp.float32
    )
    summed = summed * jnp.transpose(fade)[:, :, None] + added
    return (new_peak, total, summed)


def gradient_step(
    state, queries, query_pos, outs_back, log_total, spread, keys, values, key_pos, scale
):
    back_query, back_key, back_value = state
    scores = jnp.einsum("qhd,khd->hqk", queries, keys, preferred_element_type=jnp.float32) * scale
    allowed = (key_pos[None, :] <= query_pos[:, None])[None]
    probs = jnp.where(allowed, jnp.exp(scores - log_total[..., None]), 0.0)
    back_probs = jnp.einsum("qhd,khd->hqk", outs_back, values, preferred_element_type=jnp.float32)
    back_scores = (probs * (back_probs - spread[..., None])).astype(jnp.bfloat16)
    back_query = (
        back_query
        + jnp.einsum("hqk,khd->qhd", back_scores, keys, preferred_element_type=jnp.float32) * scale
    )
    back_key = (
        back_key
        + jnp.einsum("hqk,qhd->khd", back_scores, queries, preferred_element_type=jnp.float32)
        * scale
    )
    back_value = back_value + jnp.einsum(
        "hqk,qhd->khd", probs.astype(jnp.bfloat16), outs_back, preferred_element_type=jnp.float32
    )
    return (back_query, back_key, back_value)


def on_device(
    inputs,
    positions,
    in_weight,
    in_bias,
    out_weight,
    out_bias,
    up_weight,
    up_bias,
    down_weight,
    down_bias,
    first_gain,
    first_shift,
    second_gain,
    second_shift,
    out_grad,
):
    gathered = (
        lax.all_gather(in_weight, "fsdp", axis=0, tiled=True),
        lax.all_gather(in_bias, "fsdp", axis=0, tiled=True),
        lax.all_gather(out_weight, "fsdp", axis=0, tiled=True),
        lax.all_gather(out_bias, "fsdp", axis=0, tiled=True),
        lax.all_gather(up_weight, "fsdp", axis=0, tiled=True),
        lax.all_gather(up_bias, "fsdp", axis=0, tiled=True),
        lax.all_gather(down_weight, "fsdp", axis=0, tiled=True),
        lax.all_gather(down_bias, "fsdp", axis=0, tiled=True),
        lax.all_gather(first_gain, "fsdp", axis=0, tiled=True),
        lax.all_gather(first_shift, "fsdp", axis=0, tiled=True),
        lax.all_gather(second_gain, "fsdp", axis=0, tiled=True),
        lax.all_gather(second_shift, "fsdp", axis=0, tiled=True),
    )
    (
        full_in,
        full_in_bias,
        full_out,
        full_out_bias,
        full_up,
        full_up_bias,
        full_down,
        full_down_bias,
        gain_one,
        shift_one,
        gain_two,
        shift_two,
    ) = gathered
    tokens = inputs.shape[1]
    width = inputs.shape[2]
    heads = width // HEAD
    scale = 1.0 / math.sqrt(HEAD)
    query_pos = positions[0]
    all_pos = lax.all_gather(query_pos, "ctx", axis=0, tiled=True)
    resid = inputs[0].astype(jnp.float32)

    def norms(values, gain_a, shift_a, gain_b, shift_b):
        return (layer_norm(values, gain_a, shift_a), layer_norm(values, gain_b, shift_b))

    (normed_one, normed_two), norm_back = jax.vjp(
        norms,
        resid,
        gain_one.astype(jnp.float32),
        shift_one.astype(jnp.float32),
        gain_two.astype(jnp.float32),
        shift_two.astype(jnp.float32),
    )
    first = normed_one.astype(jnp.bfloat16)
    second = normed_two.astype(jnp.bfloat16)
    projected = jnp.dot(first, full_in, preferred_element_type=jnp.float32) + full_in_bias.astype(
        jnp.float32
    )
    projected = projected.reshape(tokens, 3, heads, HEAD)
    cosine, sine = turn_tables(query_pos)
    queries = rotate(projected[:, 0], cosine, sine).astype(jnp.bfloat16)
    keys = rotate(projected[:, 1], cosine, sine).astype(jnp.bfloat16)
    values = projected[:, 2].astype(jnp.bfloat16)
    start_state = (
        jnp.full((heads, tokens), NEG, jnp.float32),
        jnp.zeros((heads, tokens), jnp.float32),
        jnp.zeros((tokens, heads, HEAD), jnp.float32),
    )
    carry = start_state
    key_piece = lax.all_gather(keys, "ctx", axis=0, tiled=True)
    value_piece = lax.all_gather(values, "ctx", axis=0, tiled=True)
    count = key_piece.shape[0]
    size = 512

    def one_block(inner, offset):
        key_block = lax.dynamic_slice_in_dim(key_piece, offset, size, 0)
        value_block = lax.dynamic_slice_in_dim(value_piece, offset, size, 0)
        key_pos = lax.dynamic_slice_in_dim(all_pos, offset, size, 0)
        result = softmax_step(inner, queries, query_pos, key_block, value_block, key_pos, scale)
        return (result, None)

    carry, _ = lax.scan(one_block, carry, jnp.arange(0, count, size, dtype=jnp.int32))
    peak, total, summed = carry
    attended = summed / jnp.transpose(total)[:, :, None]
    log_total = peak + jnp.log(total)
    mixed = attended.reshape(tokens, width).astype(jnp.bfloat16)
    up = jnp.dot(second, full_up, preferred_element_type=jnp.float32) + full_up_bias.astype(
        jnp.float32
    )
    activated, gelu_back = jax.vjp(lambda value: jax.nn.gelu(value, approximate=False), up)
    activated = activated.astype(jnp.bfloat16)
    branch_attn = jnp.dot(
        mixed, full_out, preferred_element_type=jnp.float32
    ) + full_out_bias.astype(jnp.float32)
    branch_ff = jnp.dot(
        activated, full_down, preferred_element_type=jnp.float32
    ) + full_down_bias.astype(jnp.float32)
    output = resid + branch_attn + branch_ff
    cotangent = out_grad[0]
    back_out = cotangent.astype(jnp.float32)
    bias_sum = jnp.sum(back_out, 0)
    out_weight_part = across(mixed, cotangent)
    down_weight_part = across(activated, cotangent)
    back_mixed = against(cotangent, full_out).astype(jnp.bfloat16)
    back_active = against(cotangent, full_down)
    back_up = gelu_back(back_active)[0].astype(jnp.bfloat16)
    up_weight_part = across(second, back_up)
    up_bias_part = jnp.sum(back_up.astype(jnp.float32), 0)
    back_second = against(back_up, full_up)
    outs_back = back_mixed.reshape(tokens, heads, HEAD)
    spread = jnp.einsum("qhd,qhd->hq", outs_back.astype(jnp.float32), attended)
    cycle_size = lax.axis_size("ctx")
    here = lax.axis_index("ctx")
    zeros = jnp.zeros((tokens, heads, HEAD), jnp.float32)

    def key_turn(turn, state):
        moving_key, moving_value, back_key, back_value, back_query = state
        owner = (here - turn) % cycle_size
        key_pos = lax.dynamic_slice_in_dim(all_pos, owner * tokens, tokens, 0)
        back_query, back_key, back_value = gradient_step(
            (back_query, back_key, back_value),
            queries,
            query_pos,
            outs_back,
            log_total,
            spread,
            moving_key,
            moving_value,
            key_pos,
            scale,
        )
        moving_key, moving_value = from_behind((moving_key, moving_value), "ctx", 1)
        back_key, back_value = (
            from_behind(back_key.astype(jnp.bfloat16), "ctx", 1).astype(back_key.dtype),
            from_behind(back_value.astype(jnp.bfloat16), "ctx", 1).astype(back_value.dtype),
        )
        return (moving_key, moving_value, back_key, back_value, back_query)

    final = lax.fori_loop(0, cycle_size, key_turn, (keys, values, zeros, zeros, zeros))
    back_query, back_key, back_value = (final[4], final[2], final[3])
    back_query = rotate(back_query, cosine, -sine)
    back_key = rotate(back_key, cosine, -sine)
    back_projected = (
        jnp.stack([back_query, back_key, back_value], 1)
        .reshape(tokens, 3 * width)
        .astype(jnp.bfloat16)
    )
    in_weight_part = across(first, back_projected)
    in_bias_part = jnp.sum(back_projected.astype(jnp.float32), 0)
    back_first = against(back_projected, full_in)
    back_resid, gain_one_part, shift_one_part, gain_two_part, shift_two_part = norm_back(
        (back_first, back_second)
    )
    input_gradient = back_out + back_resid
    shares = (
        lax.psum_scatter(
            in_weight_part.astype(jnp.bfloat16), "fsdp", scatter_dimension=0, tiled=True
        ).astype(jnp.float32),
        lax.psum_scatter(
            in_bias_part.astype(jnp.bfloat16), "fsdp", scatter_dimension=0, tiled=True
        ).astype(jnp.float32),
        lax.psum_scatter(
            out_weight_part.astype(jnp.bfloat16), "fsdp", scatter_dimension=0, tiled=True
        ).astype(jnp.float32),
        lax.psum_scatter(
            bias_sum.astype(jnp.bfloat16), "fsdp", scatter_dimension=0, tiled=True
        ).astype(jnp.float32),
        lax.psum_scatter(
            up_weight_part.astype(jnp.bfloat16), "fsdp", scatter_dimension=0, tiled=True
        ).astype(jnp.float32),
        lax.psum_scatter(
            up_bias_part.astype(jnp.bfloat16), "fsdp", scatter_dimension=0, tiled=True
        ).astype(jnp.float32),
        lax.psum_scatter(
            down_weight_part.astype(jnp.bfloat16), "fsdp", scatter_dimension=0, tiled=True
        ).astype(jnp.float32),
        lax.psum_scatter(
            gain_one_part.astype(jnp.bfloat16), "fsdp", scatter_dimension=0, tiled=True
        ).astype(jnp.float32),
        lax.psum_scatter(
            shift_one_part.astype(jnp.bfloat16), "fsdp", scatter_dimension=0, tiled=True
        ).astype(jnp.float32),
        lax.psum_scatter(
            gain_two_part.astype(jnp.bfloat16), "fsdp", scatter_dimension=0, tiled=True
        ).astype(jnp.float32),
        lax.psum_scatter(
            shift_two_part.astype(jnp.bfloat16), "fsdp", scatter_dimension=0, tiled=True
        ).astype(jnp.float32),
    )
    totals = (
        lax.psum(shares[0].astype(jnp.bfloat16), "ctx").astype(jnp.float32),
        lax.psum(shares[1].astype(jnp.bfloat16), "ctx").astype(jnp.float32),
        lax.psum(shares[2].astype(jnp.bfloat16), "ctx").astype(jnp.float32),
        lax.psum(shares[3].astype(jnp.bfloat16), "ctx").astype(jnp.float32),
        lax.psum(shares[4].astype(jnp.bfloat16), "ctx").astype(jnp.float32),
        lax.psum(shares[5].astype(jnp.bfloat16), "ctx").astype(jnp.float32),
        lax.psum(shares[6].astype(jnp.bfloat16), "ctx").astype(jnp.float32),
        lax.psum(shares[7].astype(jnp.bfloat16), "ctx").astype(jnp.float32),
        lax.psum(shares[8].astype(jnp.bfloat16), "ctx").astype(jnp.float32),
        lax.psum(shares[9].astype(jnp.bfloat16), "ctx").astype(jnp.float32),
        lax.psum(shares[10].astype(jnp.bfloat16), "ctx").astype(jnp.float32),
    )
    return (
        output.astype(jnp.bfloat16)[None],
        input_gradient[None],
        totals[0],
        totals[1],
        totals[2],
        totals[3],
        totals[4],
        totals[5],
        totals[6],
        totals[3],
        totals[7],
        totals[8],
        totals[9],
        totals[10],
    )


def solution(mesh):
    return jax.shard_map(
        on_device,
        mesh=mesh,
        in_specs=(
            P("fsdp", "ctx", None),
            P("fsdp", "ctx"),
            P("fsdp", None),
            P("fsdp"),
            P("fsdp", None),
            P("fsdp"),
            P("fsdp", None),
            P("fsdp"),
            P("fsdp", None),
            P("fsdp"),
            P("fsdp"),
            P("fsdp"),
            P("fsdp"),
            P("fsdp"),
            P("fsdp", "ctx", None),
        ),
        out_specs=(
            P("fsdp", "ctx", None),
            P("fsdp", "ctx", None),
            P("fsdp", None),
            P("fsdp"),
            P("fsdp", None),
            P("fsdp"),
            P("fsdp", None),
            P("fsdp"),
            P("fsdp", None),
            P("fsdp"),
            P("fsdp"),
            P("fsdp"),
            P("fsdp"),
            P("fsdp"),
        ),
        check_vma=False,
    )
```

profile of v0, /device:TPU:0, one launch (start us, length us, event | category | flops | bytes accessed | tf_op | source)
XLA Modules:
  0.0 707.0 jit_solution(10681487738134994407)
XLA Ops:
  14.8 18.4 %all-reduce.17 = (bf16[768]{0:T(1024)(128)(2,1)}, bf16[768]{0:T(1024)(128)(2,1)}, bf16[2304]{0:T(1024)(128)(2,1)S(1)}, bf16[768]{0:T(1024)(128)(2,1)S(1)}, bf16[768]{0:T(1024)(128)(2,1)S(1)}) all-reduce(bf16[768]{0:T(1024)(128)(2,1)S(1)} %dynamic-update-slice.5, ...), channel_id=1, replica_groups=mesh['fsdp'=4,'ctx'=8] {'fsdp'}, use_global_device_ids=true, to_apply=%add.5 | all-reduce | flops 5376 | bytes 21504
  37.1 22.8 %all-gather.10.cloned.1.call-done = bf16[768,2304]{1,0:T(8,128)(2,1)} async-done(((bf16[192,2304]{1,0:T(8,128)(2,1)}), bf16[768,2304]{1,0:T(8,128)(2,1)}) %all-gather.10.cloned.1.call-update) | async-done | bytes 3538960 | tf_op jit(solution)/shard_map/all_gather | solution.py:109
  59.9 4.7 convolution_add_fusion
  71.0 12.8 %all-gather = s32[1,2048]{1,0:T(1,128)} all-gather(s32[1,256]{1,0:T(1,128)} %param.20), channel_id=2, replica_groups=mesh['fsdp'=4,'ctx'=8] {'ctx'}, dimensions={1}, use_global_device_ids=true | all-gather | bytes 9216 | tf_op jit(solution)/shard_map/all_gather | solution.py:141
  85.9 8.1 %all-gather.2 = bf16[4,1,768]{2,1,0:T(2,128)(2,1)S(1)} all-gather(bf16[1,1,768]{2,1,0:T(2,128)(2,1)S(1)} %reshape.293), channel_id=1, replica_groups=mesh['fsdp'=4,'ctx'=8] {'fsdp'}, dimensions={0}, use_global_device_ids=true | all-gather | bytes 7680 | tf_op jit(solution)/shard_map/all_gather | solution.py:114
  94.1 13.7 %all-gather.12.cloned.1.call-done = bf16[2048,12,64]{0,2,1:T(8,128)(2,1)} async-done(((bf16[256,12,64]{0,2,1:T(8,128)(2,1)}), bf16[2048,12,64]{0,2,1:T(8,128)(2,1)}) %all-gather.12.cloned.1.call-update) | async-done | bytes 3145744 | tf_op jit(solution)/shard_map/all_gather | solution.py:171
  107.7 41.4 %all-gather.20.cloned.1.call-done = bf16[2048,1,12,64]{0,3,2,1:T(8,128)(2,1)} async-done(((bf16[256,1,12,64]{0,3,2,1:T(8,128)(2,1)}), bf16[2048,1,12,64]{0,3,2,1:T(8,128)(2,1)}) %all-gather.20.cloned.1.call-update) | async-done | bytes 3145744 | tf_op jit(solution)/shard_map/all_gather | solution.py:172
  149.1 64.1 %while.39 = (s32[]{:T(128)}, f32[12,256]{1,0:T(8,128)S(1)}, f32[12,256]{1,0:T(8,128)S(1)}, f32[256,12,64]{0,2,1:T(8,128)S(1)}, s32[4]{0:T(128)S(1)}, /*index=5*/...) while((s32[]{:T(128)}, f32[12,256]{1,0:T(8,128)S(1)}, ...), condition=%wide.region_5.6_spmd.clone, body=%wide.region_2.5_spmd.clone.sunk | while | flops 420694016 | bytes 48307420 | solution.py:183
  153.2 5.7 fusion.173
  158.9 4.8 fusion.177
  169.2 5.5 fusion.173
  174.7 4.8 fusion.177
  185.8 5.5 fusion.173
  191.3 4.8 fusion.177
  201.6 5.4 fusion.173
  207.1 4.7 fusion.177
  215.2 11.6 %multiply_convert_fusion.1 = (bf16[256,3072]{1,0:T(8,128)(2,1)S(1)}, f32[256,3072]{1,0:T(8,128)}, f32[256,3072]{1,0:T(8,128)}) fusion(f32[3072]{0:T(1024)S(1)} %bitcast.232, bf16[768,3072]{1,0:T(8,128)(2,1)} %all-gather.16.cloned.1.call-done, bf16[1,256,768]{2,1,0:T(8,128)(2,1)S(1)} %copy-done.3, f32[768]{0:T(1024)S(1)} %convert_element_type.251, ...), kind=kOutput, calls=%fused_computation.54 | convolution fusion | flops 1261043712 | bytes 12996608 | tf_op jit(solution)/shard_map/dot_general | solution.py:188
  226.7 38.2 %all-gather.18.cloned.1.call-done = bf16[3072,768]{1,0:T(8,128)(2,1)} async-done(((bf16[768,768]{1,0:T(8,128)(2,1)}), bf16[3072,768]{1,0:T(8,128)(2,1)}) %all-gather.18.cloned.1.call-update) | async-done | bytes 4718608 | tf_op jit(solution)/shard_map/all_gather | solution.py:115
  264.9 6.8 fusion.119
  272.9 3.7 convolution_convert_fusion.1
  276.7 17.6 %all-gather.14.cloned.1.call-done = bf16[768,768]{1,0:T(8,128)(2,1)} async-done(((bf16[192,768]{1,0:T(8,128)(2,1)}), bf16[768,768]{1,0:T(8,128)(2,1)}) %all-gather.14.cloned.1.call-update) | async-done | bytes 1179664 | tf_op jit(solution)/shard_map/all_gather | solution.py:111
  294.4 2.5 convolution_convert_fusion.4
  300.7 3.5 convolution_convert_fusion
  307.7 244.7 %while.40 = (s32[]{:T(128)}, bf16[256,12,64]{0,2,1:T(8,128)(2,1)}, bf16[256,12,64]{0,2,1:T(8,128)(2,1)}, f32[256,12,64]{0,2,1:T(8,128)S(1)}, f32[256,12,64]{0,2,...) while((s32[]{:T(128)}, bf16[256,12,64]{0,2,1:T(8,128)(2,1)}, ...), condition=%wide.region_9.10_spmd.clone, body=%wide.region_8.9_spmd.clone.sunk | while | flops 513605632 | bytes 40837772 | solution.py:240
  316.4 2.6 fusion.190
  326.8 3.1 collective-permute-done.3
  334.1 4.2 collective-permute-done.1
  346.9 2.6 fusion.190
  352.6 3.6 collective-permute-done.2
  357.3 3.1 collective-permute-done.3
  364.7 4.2 collective-permute-done.1
  377.6 2.6 fusion.190
  381.9 5.1 collective-permute-done.2
  388.0 3.1 collective-permute-done.3
  395.4 4.2 collective-permute-done.1
  404.6 2.5 multiply_convert_fusion.3
  408.2 2.7 fusion.190
  412.6 5.0 collective-permute-done.2
  418.6 3.1 collective-permute-done.3
  426.0 4.2 collective-permute-done.1
  438.8 2.6 fusion.190
  443.1 5.1 collective-permute-done.2
  449.2 3.1 collective-permute-done.3
  456.6 4.2 collective-permute-done.1
  469.4 2.6 fusion.190
  473.6 5.1 collective-permute-done.2
  479.8 3.1 collective-permute-done.3
  487.1 4.2 collective-permute-done.1
  499.9 2.6 fusion.190
  504.2 5.1 collective-permute-done.2
  510.3 3.1 collective-permute-done.3
  517.7 4.2 collective-permute-done.1
  530.5 2.6 fusion.190
  534.7 5.1 collective-permute-done.2
  540.9 3.1 collective-permute-done.3
  548.2 4.2 collective-permute-done.1
  556.2 3.2 convolution_convert_fusion.2
  563.0 4.8 fusion.121
  570.0 34.4 %reduce-scatter.5.cloned.1.call-done = bf16[192,2304]{1,0:T(8,128)(2,1)} async-done(((bf16[768,2304]{1,0:T(8,128)(2,1)}), bf16[192,2304]{1,0:T(8,128)(2,1)}) %reduce-scatter.5.cloned.1.call-update) | async-done | bytes 884752 | tf_op jit(solution)/shard_map/reduce_scatter | solution.py:257
  606.4 15.3 %all-reduce.16 = (bf16[768]{0:T(1024)(128)(2,1)S(1)}, bf16[768]{0:T(1024)(128)(2,1)S(1)}, bf16[2304]{0:T(1024)(128)(2,1)S(1)}, bf16[768]{0:T(1024)(128)(2,1)S(1)...) all-reduce(bf16[768]{0:T(1024)(128)(2,1)S(1)} %dynamic-update-slice, ...), channel_id=1, replica_groups=mesh['fsdp'=4,'ctx'=8] {'fsdp'}, use_global_device_ids=true, to_apply=%add.6 | all-reduce | flops 10752 | bytes 43008
  622.3 15.3 %all-reduce.14 = (bf16[576]{0:T(1024)(128)(2,1)S(1)}, bf16[192]{0:T(256)(128)(2,1)S(1)}, bf16[768]{0:T(1024)(128)(2,1)S(1)}, bf16[192]{0:T(256)(128)(2,1)S(1)}, ...) all-reduce(bf16[576]{0:T(1024)(128)(2,1)S(1)} %dynamic-slice.8, ...), channel_id=1, replica_groups=mesh['fsdp'=4,'ctx'=8] {'ctx'}, use_global_device_ids=true, to_apply=%region_16.17 | all-reduce | flops 2304 | bytes 9216 | tf_op jit(solution)/shard_map/psum | solution.py:293
  641.1 3.9 convolution_add_fusion.3
  647.7 45.3 %all-reduce.20.cloned.1.call-done = (bf16[192,2304]{1,0:T(8,128)(2,1)}, bf16[192,768]{1,0:T(8,128)(2,1)}, bf16[192,3072]{1,0:T(8,128)(2,1)}, bf16[768,768]{1,0:T(8,128)(2,1)}) async-done(((bf16[192,2304]{1,0:T(8,128)(2,1)}, bf16[192,768]{1,0:T(8,128)(2,1)}, bf16[192,3072]{1,0:T(8,128)(2,1)}, bf16[768,768]{1,0:T(8,128)(2,1)}), (bf16[192,2304]{1,0:T(8,128)(2,1)}, bf16[192,768]{1,0:T(8,128)(2,1)}, ...) | async-done | bytes 3538960 | tf_op jit(solution)/shard_map/psum | solution.py:292
  693.0 3.1 convert_element_type.271
  (434 shorter events, 191.8 us)
Async XLA Ops:
  7.2 52.8 %all-gather.10.cloned.1.call-start = ((), (), s32[]{:S(2)}) async-start(), calls=%async_computation.4 | async-start | bytes 4423680 | tf_op jit(solution)/shard_map/all_gather | solution.py:109
  7.9 99.8 %all-gather.12.cloned.1.call-start = ((), (), s32[]{:S(2)}) async-start(), calls=%async_computation.5 | async-start | bytes 3538944 | tf_op jit(solution)/shard_map/all_gather | solution.py:171
  33.2 31.4 %copy-start.23 = (f32[768]{0:T(1024)}, f32[768]{0:T(1024)S(1)}, u32[]{:S(2)}) copy-start(f32[768]{0:T(1024)S(1)} %convert_element_type.241) | copy-start | bytes 9220
  33.2 31.4 %copy-start.29 = (f32[768]{0:T(1024)}, f32[768]{0:T(1024)S(1)}, u32[]{:S(2)}) copy-start(f32[768]{0:T(1024)S(1)} %convert_element_type.242) | copy-start | bytes 9220
  34.7 32.3 %copy-start.27 = (f32[256,16]{0,1:T(8,128)}, f32[256,16]{0,1:T(8,128)S(1)}, u32[]{:S(2)}) copy-start(f32[256,16]{0,1:T(8,128)S(1)} %get-tuple-element.582) | copy-start | bytes 49156
  35.8 28.8 %copy-start.32 = (f32[256]{0:T(256)}, f32[256]{0:T(256)S(1)}, u32[]{:S(2)}) copy-start(f32[256]{0:T(256)S(1)} %broadcast_multiply_fusion.1) | copy-start | bytes 3076
  37.1 27.6 %copy-start.40 = (f32[256]{0:T(256)}, f32[256]{0:T(256)S(1)}, u32[]{:S(2)}) copy-start(f32[256]{0:T(256)S(1)} %fusion.73) | copy-start | bytes 3076
  37.1 27.6 %copy-start.35 = (f32[256]{0:T(256)}, f32[256]{0:T(256)S(1)}, u32[]{:S(2)}) copy-start(f32[256]{0:T(256)S(1)} %fusion.108) | copy-start | bytes 3076
  68.4 80.7 %all-gather.20.cloned.1.call-start = ((), (), s32[]{:S(2)}) async-start(), calls=%async_computation.13 | async-start | bytes 3538944 | tf_op jit(solution)/shard_map/all_gather | solution.py:172
  69.2 145.9 %all-gather.16.cloned.1.call-start = ((), (), s32[]{:S(2)}) async-start(), calls=%async_computation.7 | async-start | bytes 5898240 | tf_op jit(solution)/shard_map/all_gather | solution.py:113
  69.8 195.1 %all-gather.18.cloned.1.call-start = ((), (), s32[]{:S(2)}) async-start(), calls=%async_computation.8 | async-start | bytes 5898240 | tf_op jit(solution)/shard_map/all_gather | solution.py:115
  70.4 223.9 %all-gather.14.cloned.1.call-start = ((), (), s32[]{:S(2)}) async-start(), calls=%async_computation.6 | async-start | bytes 1474560 | tf_op jit(solution)/shard_map/all_gather | solution.py:111
  71.0 499.0 %reduce-scatter.7.cloned.1.call-start = ((), (), s32[]{:S(2)}) async-start(), calls=%async_computation.10 | async-start | bytes 1474560 | tf_op jit(solution)/shard_map/reduce_scatter | solution.py:263
  84.5 187.2 %copy-start.25 = (f32[768]{0:T(1024)}, f32[768]{0:T(1024)S(1)}, u32[]{:S(2)}) copy-start(f32[768]{0:T(1024)S(1)} %convert_element_type.250) | copy-start | bytes 9220
  149.1 64.3 %copy-start.4 = (bf16[1,256,768]{2,1,0:T(8,128)(2,1)S(1)}, bf16[1,256,768]{2,1,0:T(8,128)(2,1)}, u32[]{:S(2)}) copy-start(bf16[1,256,768]{2,1,0:T(8,128)(2,1)} %param.33) | copy-start | bytes 1179652
  158.9 4.9 copy-start
  174.7 5.7 copy-start
  191.3 4.9 copy-start
  207.0 4.8 copy-start
  213.2 13.5 %copy-start.17 = (f32[12,256]{1,0:T(8,128)}, f32[12,256]{1,0:T(8,128)S(1)}, u32[]{:S(2)}) copy-start(f32[12,256]{1,0:T(8,128)S(1)} %get-tuple-element.380) | copy-start | bytes 36868
  213.3 13.4 %copy-start.8 = (bf16[256,12,64]{0,2,1:T(8,128)(2,1)}, bf16[256,12,64]{0,2,1:T(8,128)(2,1)S(1)}, u32[]{:S(2)}) copy-start(bf16[256,12,64]{0,2,1:T(8,128)(2,1)S(1)} %fusion.99) | copy-start | bytes 1179652
  214.9 355.1 %reduce-scatter.9.cloned.1.call-start = ((), (), s32[]{:S(2)}) async-start(), calls=%async_computation.11 | async-start | bytes 5898240 | tf_op jit(solution)/shard_map/reduce_scatter | solution.py:269
  226.7 74.0 %copy-start.10 = (bf16[256,3072]{1,0:T(8,128)(2,1)}, bf16[256,3072]{1,0:T(8,128)(2,1)S(1)}, u32[]{:S(2)}) copy-start(bf16[256,3072]{1,0:T(8,128)(2,1)S(1)} %get-tuple-element.560) | copy-start | bytes 4718596
  276.6 293.4 %reduce-scatter.11.cloned.1.call-start = ((), (), s32[]{:S(2)}) async-start(), calls=%async_computation.12 | async-start | bytes 5898240 | tf_op jit(solution)/shard_map/reduce_scatter | solution.py:275
  304.3 300.2 %reduce-scatter.5.cloned.1.call-start = ((), (), s32[]{:S(2)}) async-start(), calls=%async_computation.9 | async-start | bytes 4423680 | tf_op jit(solution)/shard_map/reduce_scatter | solution.py:257
  307.7 247.0 %copy-start.28 = (f32[256,16]{0,1:T(8,128)S(1)}, f32[256,16]{0,1:T(8,128)}, u32[]{:S(2)}) copy-start(f32[256,16]{0,1:T(8,128)} %copy-done.27) | copy-start | bytes 49156
  316.4 5.8 copy-start.1
  316.4 9.3 %collective-permute-start.2 = (bf16[256,12,64]{0,2,1:T(8,128)(2,1)}, bf16[256,12,64]{0,2,1:T(8,128)(2,1)}, u32[]{:S(2)}, u32[]{:S(2)}) collective-permute-start(bf16[256,12,64]{0,2,1:T(8,128)(2,1)} %fusion.189), channel_id=1, source_target_pairs={{0,1},{1,2},{2,3},{3,4},{4,5},{5,6},{6,7},{7,0},{8,9},{9,10},{10,1... | collective-permute-start | bytes 1179656 | tf_op jit(solution)/shard_map/while/body/eval_jaxpr/ppermute | solution.py:15
  319.0 10.9 %collective-permute-start.3 = (bf16[256,12,64]{0,2,1:T(8,128)(2,1)}, bf16[256,12,64]{0,2,1:T(8,128)(2,1)}, u32[]{:S(2)}, u32[]{:S(2)}) collective-permute-start(bf16[256,12,64]{0,2,1:T(8,128)(2,1)} %fusion.190), channel_id=1, source_target_pairs={{0,1},{1,2},{2,3},{3,4},{4,5},{5,6},{6,7},{7,0},{8,9},{9,10},{10,1... | collective-permute-start | bytes 1179656 | tf_op jit(solution)/shard_map/while/body/eval_jaxpr/ppermute | solution.py:15
  320.5 13.6 %collective-permute-start = (bf16[256,12,64]{0,2,1:T(8,128)(2,1)S(1)}, bf16[256,12,64]{0,2,1:T(8,128)(2,1)}, u32[]{:S(2)}, u32[]{:S(2)}) collective-permute-start(bf16[256,12,64]{0,2,1:T(8,128)(2,1)S(1)} %copy.76), channel_id=1, source_target_pairs={{0,1},{1,2},{2,3},{3,4},{4,5},{5,6},{6,7},{7,0},{8,9},{9,10},{10,1... | collective-permute-start | bytes 1179656 | tf_op jit(solution)/shard_map/while/body/eval_jaxpr/ppermute | solution.py:15
  320.6 17.7 %collective-permute-start.1 = (bf16[256,12,64]{0,2,1:T(8,128)(2,1)}, bf16[256,12,64]{0,2,1:T(8,128)(2,1)}, u32[]{:S(2)}, u32[]{:S(2)}) collective-permute-start(bf16[256,12,64]{0,2,1:T(8,128)(2,1)} %copy.77), channel_id=1, source_target_pairs={{0,1},{1,2},{2,3},{3,4},{4,5},{5,6},{6,7},{7,0},{8,9},{9,10},{10,1... | collective-permute-start | bytes 1179656 | tf_op jit(solution)/shard_map/while/body/eval_jaxpr/ppermute | solution.py:15
  346.9 9.3 %collective-permute-start.2 = (bf16[256,12,64]{0,2,1:T(8,128)(2,1)}, bf16[256,12,64]{0,2,1:T(8,128)(2,1)}, u32[]{:S(2)}, u32[]{:S(2)}) collective-permute-start(bf16[256,12,64]{0,2,1:T(8,128)(2,1)} %fusion.189), channel_id=1, source_target_pairs={{0,1},{1,2},{2,3},{3,4},{4,5},{5,6},{6,7},{7,0},{8,9},{9,10},{10,1... | collective-permute-start | bytes 1179656 | tf_op jit(solution)/shard_map/while/body/eval_jaxpr/ppermute | solution.py:15
  349.6 10.9 %collective-permute-start.3 = (bf16[256,12,64]{0,2,1:T(8,128)(2,1)}, bf16[256,12,64]{0,2,1:T(8,128)(2,1)}, u32[]{:S(2)}, u32[]{:S(2)}) collective-permute-start(bf16[256,12,64]{0,2,1:T(8,128)(2,1)} %fusion.190), channel_id=1, source_target_pairs={{0,1},{1,2},{2,3},{3,4},{4,5},{5,6},{6,7},{7,0},{8,9},{9,10},{10,1... | collective-permute-start | bytes 1179656 | tf_op jit(solution)/shard_map/while/body/eval_jaxpr/ppermute | solution.py:15
  349.6 15.1 %collective-permute-start = (bf16[256,12,64]{0,2,1:T(8,128)(2,1)S(1)}, bf16[256,12,64]{0,2,1:T(8,128)(2,1)}, u32[]{:S(2)}, u32[]{:S(2)}) collective-permute-start(bf16[256,12,64]{0,2,1:T(8,128)(2,1)S(1)} %copy.76), channel_id=1, source_target_pairs={{0,1},{1,2},{2,3},{3,4},{4,5},{5,6},{6,7},{7,0},{8,9},{9,10},{10,1... | collective-permute-start | bytes 1179656 | tf_op jit(solution)/shard_map/while/body/eval_jaxpr/ppermute | solution.py:15
  349.6 19.3 %collective-permute-start.1 = (bf16[256,12,64]{0,2,1:T(8,128)(2,1)}, bf16[256,12,64]{0,2,1:T(8,128)(2,1)}, u32[]{:S(2)}, u32[]{:S(2)}) collective-permute-start(bf16[256,12,64]{0,2,1:T(8,128)(2,1)} %copy.77), channel_id=1, source_target_pairs={{0,1},{1,2},{2,3},{3,4},{4,5},{5,6},{6,7},{7,0},{8,9},{9,10},{10,1... | collective-permute-start | bytes 1179656 | tf_op jit(solution)/shard_map/while/body/eval_jaxpr/ppermute | solution.py:15
  377.6 9.3 %collective-permute-start.2 = (bf16[256,12,64]{0,2,1:T(8,128)(2,1)}, bf16[256,12,64]{0,2,1:T(8,128)(2,1)}, u32[]{:S(2)}, u32[]{:S(2)}) collective-permute-start(bf16[256,12,64]{0,2,1:T(8,128)(2,1)} %fusion.189), channel_id=1, source_target_pairs={{0,1},{1,2},{2,3},{3,4},{4,5},{5,6},{6,7},{7,0},{8,9},{9,10},{10,1... | collective-permute-start | bytes 1179656 | tf_op jit(solution)/shard_map/while/body/eval_jaxpr/ppermute | solution.py:15
  380.3 10.9 %collective-permute-start.3 = (bf16[256,12,64]{0,2,1:T(8,128)(2,1)}, bf16[256,12,64]{0,2,1:T(8,128)(2,1)}, u32[]{:S(2)}, u32[]{:S(2)}) collective-permute-start(bf16[256,12,64]{0,2,1:T(8,128)(2,1)} %fusion.190), channel_id=1, source_target_pairs={{0,1},{1,2},{2,3},{3,4},{4,5},{5,6},{6,7},{7,0},{8,9},{9,10},{10,1... | collective-permute-start | bytes 1179656 | tf_op jit(solution)/shard_map/while/body/eval_jaxpr/ppermute | solution.py:15
  380.3 15.1 %collective-permute-start = (bf16[256,12,64]{0,2,1:T(8,128)(2,1)S(1)}, bf16[256,12,64]{0,2,1:T(8,128)(2,1)}, u32[]{:S(2)}, u32[]{:S(2)}) collective-permute-start(bf16[256,12,64]{0,2,1:T(8,128)(2,1)S(1)} %copy.76), channel_id=1, source_target_pairs={{0,1},{1,2},{2,3},{3,4},{4,5},{5,6},{6,7},{7,0},{8,9},{9,10},{10,1... | collective-permute-start | bytes 1179656 | tf_op jit(solution)/shard_map/while/body/eval_jaxpr/ppermute | solution.py:15
  380.3 19.3 %collective-permute-start.1 = (bf16[256,12,64]{0,2,1:T(8,128)(2,1)}, bf16[256,12,64]{0,2,1:T(8,128)(2,1)}, u32[]{:S(2)}, u32[]{:S(2)}) collective-permute-start(bf16[256,12,64]{0,2,1:T(8,128)(2,1)} %copy.77), channel_id=1, source_target_pairs={{0,1},{1,2},{2,3},{3,4},{4,5},{5,6},{6,7},{7,0},{8,9},{9,10},{10,1... | collective-permute-start | bytes 1179656 | tf_op jit(solution)/shard_map/while/body/eval_jaxpr/ppermute | solution.py:15
  408.2 9.3 %collective-permute-start.2 = (bf16[256,12,64]{0,2,1:T(8,128)(2,1)}, bf16[256,12,64]{0,2,1:T(8,128)(2,1)}, u32[]{:S(2)}, u32[]{:S(2)}) collective-permute-start(bf16[256,12,64]{0,2,1:T(8,128)(2,1)} %fusion.189), channel_id=1, source_target_pairs={{0,1},{1,2},{2,3},{3,4},{4,5},{5,6},{6,7},{7,0},{8,9},{9,10},{10,1... | collective-permute-start | bytes 1179656 | tf_op jit(solution)/shard_map/while/body/eval_jaxpr/ppermute | solution.py:15
  410.9 10.8 %collective-permute-start.3 = (bf16[256,12,64]{0,2,1:T(8,128)(2,1)}, bf16[256,12,64]{0,2,1:T(8,128)(2,1)}, u32[]{:S(2)}, u32[]{:S(2)}) collective-permute-start(bf16[256,12,64]{0,2,1:T(8,128)(2,1)} %fusion.190), channel_id=1, source_target_pairs={{0,1},{1,2},{2,3},{3,4},{4,5},{5,6},{6,7},{7,0},{8,9},{9,10},{10,1... | collective-permute-start | bytes 1179656 | tf_op jit(solution)/shard_map/while/body/eval_jaxpr/ppermute | solution.py:15
  410.9 15.0 %collective-permute-start = (bf16[256,12,64]{0,2,1:T(8,128)(2,1)S(1)}, bf16[256,12,64]{0,2,1:T(8,128)(2,1)}, u32[]{:S(2)}, u32[]{:S(2)}) collective-permute-start(bf16[256,12,64]{0,2,1:T(8,128)(2,1)S(1)} %copy.76), channel_id=1, source_target_pairs={{0,1},{1,2},{2,3},{3,4},{4,5},{5,6},{6,7},{7,0},{8,9},{9,10},{10,1... | collective-permute-start | bytes 1179656 | tf_op jit(solution)/shard_map/while/body/eval_jaxpr/ppermute | solution.py:15
  410.9 19.2 %collective-permute-start.1 = (bf16[256,12,64]{0,2,1:T(8,128)(2,1)}, bf16[256,12,64]{0,2,1:T(8,128)(2,1)}, u32[]{:S(2)}, u32[]{:S(2)}) collective-permute-start(bf16[256,12,64]{0,2,1:T(8,128)(2,1)} %copy.77), channel_id=1, source_target_pairs={{0,1},{1,2},{2,3},{3,4},{4,5},{5,6},{6,7},{7,0},{8,9},{9,10},{10,1... | collective-permute-start | bytes 1179656 | tf_op jit(solution)/shard_map/while/body/eval_jaxpr/ppermute | solution.py:15
  438.8 9.3 %collective-permute-start.2 = (bf16[256,12,64]{0,2,1:T(8,128)(2,1)}, bf16[256,12,64]{0,2,1:T(8,128)(2,1)}, u32[]{:S(2)}, u32[]{:S(2)}) collective-permute-start(bf16[256,12,64]{0,2,1:T(8,128)(2,1)} %fusion.189), channel_id=1, source_target_pairs={{0,1},{1,2},{2,3},{3,4},{4,5},{5,6},{6,7},{7,0},{8,9},{9,10},{10,1... | collective-permute-start | bytes 1179656 | tf_op jit(solution)/shard_map/while/body/eval_jaxpr/ppermute | solution.py:15
  441.5 10.9 %collective-permute-start.3 = (bf16[256,12,64]{0,2,1:T(8,128)(2,1)}, bf16[256,12,64]{0,2,1:T(8,128)(2,1)}, u32[]{:S(2)}, u32[]{:S(2)}) collective-permute-start(bf16[256,12,64]{0,2,1:T(8,128)(2,1)} %fusion.190), channel_id=1, source_target_pairs={{0,1},{1,2},{2,3},{3,4},{4,5},{5,6},{6,7},{7,0},{8,9},{9,10},{10,1... | collective-permute-start | bytes 1179656 | tf_op jit(solution)/shard_map/while/body/eval_jaxpr/ppermute | solution.py:15
  441.5 15.1 %collective-permute-start = (bf16[256,12,64]{0,2,1:T(8,128)(2,1)S(1)}, bf16[256,12,64]{0,2,1:T(8,128)(2,1)}, u32[]{:S(2)}, u32[]{:S(2)}) collective-permute-start(bf16[256,12,64]{0,2,1:T(8,128)(2,1)S(1)} %copy.76), channel_id=1, source_target_pairs={{0,1},{1,2},{2,3},{3,4},{4,5},{5,6},{6,7},{7,0},{8,9},{9,10},{10,1... | collective-permute-start | bytes 1179656 | tf_op jit(solution)/shard_map/while/body/eval_jaxpr/ppermute | solution.py:15
  441.5 19.3 %collective-permute-start.1 = (bf16[256,12,64]{0,2,1:T(8,128)(2,1)}, bf16[256,12,64]{0,2,1:T(8,128)(2,1)}, u32[]{:S(2)}, u32[]{:S(2)}) collective-permute-start(bf16[256,12,64]{0,2,1:T(8,128)(2,1)} %copy.77), channel_id=1, source_target_pairs={{0,1},{1,2},{2,3},{3,4},{4,5},{5,6},{6,7},{7,0},{8,9},{9,10},{10,1... | collective-permute-start | bytes 1179656 | tf_op jit(solution)/shard_map/while/body/eval_jaxpr/ppermute | solution.py:15
  469.4 9.3 %collective-permute-start.2 = (bf16[256,12,64]{0,2,1:T(8,128)(2,1)}, bf16[256,12,64]{0,2,1:T(8,128)(2,1)}, u32[]{:S(2)}, u32[]{:S(2)}) collective-permute-start(bf16[256,12,64]{0,2,1:T(8,128)(2,1)} %fusion.189), channel_id=1, source_target_pairs={{0,1},{1,2},{2,3},{3,4},{4,5},{5,6},{6,7},{7,0},{8,9},{9,10},{10,1... | collective-permute-start | bytes 1179656 | tf_op jit(solution)/shard_map/while/body/eval_jaxpr/ppermute | solution.py:15
  472.0 10.9 %collective-permute-start.3 = (bf16[256,12,64]{0,2,1:T(8,128)(2,1)}, bf16[256,12,64]{0,2,1:T(8,128)(2,1)}, u32[]{:S(2)}, u32[]{:S(2)}) collective-permute-start(bf16[256,12,64]{0,2,1:T(8,128)(2,1)} %fusion.190), channel_id=1, source_target_pairs={{0,1},{1,2},{2,3},{3,4},{4,5},{5,6},{6,7},{7,0},{8,9},{9,10},{10,1... | collective-permute-start | bytes 1179656 | tf_op jit(solution)/shard_map/while/body/eval_jaxpr/ppermute | solution.py:15
  472.0 15.1 %collective-permute-start = (bf16[256,12,64]{0,2,1:T(8,128)(2,1)S(1)}, bf16[256,12,64]{0,2,1:T(8,128)(2,1)}, u32[]{:S(2)}, u32[]{:S(2)}) collective-permute-start(bf16[256,12,64]{0,2,1:T(8,128)(2,1)S(1)} %copy.76), channel_id=1, source_target_pairs={{0,1},{1,2},{2,3},{3,4},{4,5},{5,6},{6,7},{7,0},{8,9},{9,10},{10,1... | collective-permute-start | bytes 1179656 | tf_op jit(solution)/shard_map/while/body/eval_jaxpr/ppermute | solution.py:15
  472.0 19.3 %collective-permute-start.1 = (bf16[256,12,64]{0,2,1:T(8,128)(2,1)}, bf16[256,12,64]{0,2,1:T(8,128)(2,1)}, u32[]{:S(2)}, u32[]{:S(2)}) collective-permute-start(bf16[256,12,64]{0,2,1:T(8,128)(2,1)} %copy.77), channel_id=1, source_target_pairs={{0,1},{1,2},{2,3},{3,4},{4,5},{5,6},{6,7},{7,0},{8,9},{9,10},{10,1... | collective-permute-start | bytes 1179656 | tf_op jit(solution)/shard_map/while/body/eval_jaxpr/ppermute | solution.py:15
  499.9 9.3 %collective-permute-start.2 = (bf16[256,12,64]{0,2,1:T(8,128)(2,1)}, bf16[256,12,64]{0,2,1:T(8,128)(2,1)}, u32[]{:S(2)}, u32[]{:S(2)}) collective-permute-start(bf16[256,12,64]{0,2,1:T(8,128)(2,1)} %fusion.189), channel_id=1, source_target_pairs={{0,1},{1,2},{2,3},{3,4},{4,5},{5,6},{6,7},{7,0},{8,9},{9,10},{10,1... | collective-permute-start | bytes 1179656 | tf_op jit(solution)/shard_map/while/body/eval_jaxpr/ppermute | solution.py:15
  502.6 10.9 %collective-permute-start.3 = (bf16[256,12,64]{0,2,1:T(8,128)(2,1)}, bf16[256,12,64]{0,2,1:T(8,128)(2,1)}, u32[]{:S(2)}, u32[]{:S(2)}) collective-permute-start(bf16[256,12,64]{0,2,1:T(8,128)(2,1)} %fusion.190), channel_id=1, source_target_pairs={{0,1},{1,2},{2,3},{3,4},{4,5},{5,6},{6,7},{7,0},{8,9},{9,10},{10,1... | collective-permute-start | bytes 1179656 | tf_op jit(solution)/shard_map/while/body/eval_jaxpr/ppermute | solution.py:15
  502.6 15.1 %collective-permute-start = (bf16[256,12,64]{0,2,1:T(8,128)(2,1)S(1)}, bf16[256,12,64]{0,2,1:T(8,128)(2,1)}, u32[]{:S(2)}, u32[]{:S(2)}) collective-permute-start(bf16[256,12,64]{0,2,1:T(8,128)(2,1)S(1)} %copy.76), channel_id=1, source_target_pairs={{0,1},{1,2},{2,3},{3,4},{4,5},{5,6},{6,7},{7,0},{8,9},{9,10},{10,1... | collective-permute-start | bytes 1179656 | tf_op jit(solution)/shard_map/while/body/eval_jaxpr/ppermute | solution.py:15
  502.6 19.3 %collective-permute-start.1 = (bf16[256,12,64]{0,2,1:T(8,128)(2,1)}, bf16[256,12,64]{0,2,1:T(8,128)(2,1)}, u32[]{:S(2)}, u32[]{:S(2)}) collective-permute-start(bf16[256,12,64]{0,2,1:T(8,128)(2,1)} %copy.77), channel_id=1, source_target_pairs={{0,1},{1,2},{2,3},{3,4},{4,5},{5,6},{6,7},{7,0},{8,9},{9,10},{10,1... | collective-permute-start | bytes 1179656 | tf_op jit(solution)/shard_map/while/body/eval_jaxpr/ppermute | solution.py:15
  530.5 9.3 %collective-permute-start.2 = (bf16[256,12,64]{0,2,1:T(8,128)(2,1)}, bf16[256,12,64]{0,2,1:T(8,128)(2,1)}, u32[]{:S(2)}, u32[]{:S(2)}) collective-permute-start(bf16[256,12,64]{0,2,1:T(8,128)(2,1)} %fusion.189), channel_id=1, source_target_pairs={{0,1},{1,2},{2,3},{3,4},{4,5},{5,6},{6,7},{7,0},{8,9},{9,10},{10,1... | collective-permute-start | bytes 1179656 | tf_op jit(solution)/shard_map/while/body/eval_jaxpr/ppermute | solution.py:15
  533.1 10.9 %collective-permute-start.3 = (bf16[256,12,64]{0,2,1:T(8,128)(2,1)}, bf16[256,12,64]{0,2,1:T(8,128)(2,1)}, u32[]{:S(2)}, u32[]{:S(2)}) collective-permute-start(bf16[256,12,64]{0,2,1:T(8,128)(2,1)} %fusion.190), channel_id=1, source_target_pairs={{0,1},{1,2},{2,3},{3,4},{4,5},{5,6},{6,7},{7,0},{8,9},{9,10},{10,1... | collective-permute-start | bytes 1179656 | tf_op jit(solution)/shard_map/while/body/eval_jaxpr/ppermute | solution.py:15
  533.1 15.1 %collective-permute-start = (bf16[256,12,64]{0,2,1:T(8,128)(2,1)S(1)}, bf16[256,12,64]{0,2,1:T(8,128)(2,1)}, u32[]{:S(2)}, u32[]{:S(2)}) collective-permute-start(bf16[256,12,64]{0,2,1:T(8,128)(2,1)S(1)} %copy.76), channel_id=1, source_target_pairs={{0,1},{1,2},{2,3},{3,4},{4,5},{5,6},{6,7},{7,0},{8,9},{9,10},{10,1... | collective-permute-start | bytes 1179656 | tf_op jit(solution)/shard_map/while/body/eval_jaxpr/ppermute | solution.py:15
  533.1 19.3 %collective-permute-start.1 = (bf16[256,12,64]{0,2,1:T(8,128)(2,1)}, bf16[256,12,64]{0,2,1:T(8,128)(2,1)}, u32[]{:S(2)}, u32[]{:S(2)}) collective-permute-start(bf16[256,12,64]{0,2,1:T(8,128)(2,1)} %copy.77), channel_id=1, source_target_pairs={{0,1},{1,2},{2,3},{3,4},{4,5},{5,6},{6,7},{7,0},{8,9},{9,10},{10,1... | collective-permute-start | bytes 1179656 | tf_op jit(solution)/shard_map/while/body/eval_jaxpr/ppermute | solution.py:15
  559.5 133.5 %all-reduce.20.cloned.1.call-start = ((), (), s32[]{:S(2)}) async-start(), calls=%async_computation.14 | async-start | bytes 7077888 | tf_op jit(solution)/shard_map/psum | solution.py:292
  563.0 4.8 copy-start.44
  569.9 36.5 %copy-start.42 = (bf16[3072]{0:T(1024)(128)(2,1)S(1)}, bf16[3072]{0:T(1024)(128)(2,1)}, u32[]{:S(2)}) copy-start(bf16[3072]{0:T(1024)(128)(2,1)} %get-tuple-element.586) | copy-start | bytes 18436
  569.9 71.1 %copy-start.11 = (bf16[256,3072]{1,0:T(8,128)(2,1)S(1)}, bf16[256,3072]{1,0:T(8,128)(2,1)}, u32[]{:S(2)}) copy-start(bf16[256,3072]{1,0:T(8,128)(2,1)} %copy-done.10) | copy-start | bytes 4718596
  638.8 61.1 %copy-start.43 = (f32[192]{0:T(256)}, f32[192]{0:T(256)S(1)}, u32[]{:S(2)}) copy-start(f32[192]{0:T(256)S(1)} %convert_element_type.269) | copy-start | bytes 2308
  (64 other events, 133.2 us)
Sparse Core Ops, SparseCore 0:
  9.9 50.0 all-gather.9
  68.5 39.1 all-gather.11
  109.9 39.1 all-gather.19
  150.8 55.2 all-gather.15
  207.8 57.0 all-gather.17
  266.6 27.7 all-gather.13
  297.3 28.5 reduce-scatter.6
  328.8 57.0 reduce-scatter.8
  388.9 57.0 reduce-scatter.10
  559.6 44.8 reduce-scatter.4
  607.1 85.8 all-reduce.19
where the time goes:
time: 711 us; the launch traced here: 707 us
  waiting for transfers between devices  329 us (46%)
  matrix products  151 us (21%)
  blocking collectives  69.9 us (10%)
  other arithmetic  63.4 us (9%)
  local copies, waits for them, and re-layouts  62.1 us (9%)
  between operations  17.8 us (3%)
  loops' own time  8.68 us (1%)
    ppermute x32, waiting for transfers between devices, from_behind(): return lax.ppermute(x, axis, [(i, (i + by) % size) for i in range(size)])  113 us
    psum x1, waiting for transfers between devices, on_device(): lax.psum(shares[0].astype(jnp.bfloat16), 'ctx').astype(jnp.float32)  45.3 us
    all_gather x1, waiting for transfers between devices, on_device(): value_piece = lax.all_gather(values, 'ctx', axis=0, tiled=True)  41.4 us
    all_gather x1, waiting for transfers between devices, on_device(): lax.all_gather(down_weight, 'fsdp', axis=0, tiled=True)  38.2 us
    reduce_scatter x1, waiting for transfers between devices, on_device(): lax.psum_scatter(in_weight_part.astype(jnp.bfloat16), 'fsdp', scatter_dim...  34.4 us
    unnamed x2, blocking collectives  33.7 us
    while x108, local copies, waits for them, and re-layouts  31 us
    all_gather x1, waiting for transfers between devices, on_device(): lax.all_gather(in_weight, 'fsdp', axis=0, tiled=True)  22.8 us
  transfers between devices with their start and end apart: 43, of which 39 were waited for; matrix products, arithmetic and copies ran while one was open for 35% of the time, Pallas kernels for 0%

commit v1 on v0

--- a/solution.py
+++ b/solution.py
@@ -8,6 +8,22 @@
 ROT = 16
 NEG = -1e30
 EPS = 1e-05
+
+
+def collect(x, axis, dim):
+    ways, here, step = (lax.axis_size(axis), lax.axis_index(axis), x.shape[dim])
+    lengths = [n * ways if d == dim else n for d, n in enumerate(x.shape)]
+    full = lax.dynamic_update_slice_in_dim(jnp.zeros(lengths, x.dtype), x, here * step, axis=dim)
+    going_up = going_down = x
+    for far in range(1, ways // 2 + 1):
+        going_up = lax.ppermute(going_up, axis, [(d, (d + 1) % ways) for d in range(ways)])
+        full = lax.dynamic_update_slice_in_dim(full, going_up, (here - far) % ways * step, axis=dim)
+        if 2 * far < ways:
+            going_down = lax.ppermute(going_down, axis, [(d, (d - 1) % ways) for d in range(ways)])
+            full = lax.dynamic_update_slice_in_dim(
+                full, going_down, (here + far) % ways * step, axis=dim
+            )
+    return full
 
 
 def from_behind(x, axis, by):
@@ -169,7 +185,7 @@
     )
     carry = start_state
     key_piece = lax.all_gather(keys, "ctx", axis=0, tiled=True)
-    value_piece = lax.all_gather(values, "ctx", axis=0, tiled=True)
+    value_piece = collect(values, "ctx", 0)
     count = key_piece.shape[0]
     size = 512
 

time: 711 us -> 686 us (0.965)
  waiting for transfers between devices: 329 us -> 271 us
  blocking collectives: 69.9 us -> 79.9 us
  starting transfers between devices: 5.51 us -> 15.3 us
  local copies, waits for them, and re-layouts: 62.1 us -> 70.7 us
    all_gather x1 -> x0, waiting for transfers between devices: 41.4 us -> none  [on_device(): value_piece = lax.all_gather(values, 'ctx', axis=0, tiled=True)]
    all_gather x1, waiting for transfers between devices: 38.2 us -> 7.83 us  [on_device(): lax.all_gather(down_weight, 'fsdp', axis=0, tiled=True)]
    ppermute x0 -> x7, waiting for transfers between devices: none -> 28.2 us  [the longest x4 20.7 us: collect(): lax.ppermute(going_up, axis, [(d, (d + 1) % ways) for d in range(ways)])]
    all_gather x1, waiting for transfers between devices: 13.7 us -> 0.01 us  [on_device(): key_piece = lax.all_gather(keys, 'ctx', axis=0, tiled=True)]
    ppermute x0 -> x7, starting transfers between devices: none -> 10.1 us  [the longest x3 9.6 us: collect(): lax.ppermute(going_down, axis, [(d, (d - 1) % ways) for d in range(ways)])]
    dynamic_update_slice x0 -> x8, local copies, waits for them, and re-layouts: none -> 9.79 us  [the longest x4 5.38 us: collect(): lax.dynamic_update_slice_in_dim(full, going_up, (here - far) % ways * ste...]
    all_gather x1, blocking collectives: 12.8 us -> 22.5 us  [on_device(): all_pos = lax.all_gather(query_pos, 'ctx', axis=0, tiled=True)]
  transfers between devices with their start and end apart: 43 -> 49, of which waited for: 39 -> 42; matrix products, arithmetic and copies ran while one was open for 35% -> 38% of each run, Pallas kernels for 0% -> 0%
where the time goes in v1:
time: 686 us; the launch traced here: 682 us
  waiting for transfers between devices  271 us (40%)
  matrix products  151 us (22%)
  blocking collectives  79.9 us (12%)
  local copies, waits for them, and re-layouts  70.7 us (10%)
  other arithmetic  67.3 us (10%)
  between operations  18.1 us (3%)
  starting transfers between devices  15.3 us (2%)
  loops' own time  8.69 us (1%)
    ppermute x32, waiting for transfers between devices, from_behind(): return lax.ppermute(x, axis, [(i, (i + by) % size) for i in range(size)])  113 us
    psum x1, waiting for transfers between devices, on_device(): lax.psum(shares[0].astype(jnp.bfloat16), 'ctx').astype(jnp.float32)  45.1 us
    reduce_scatter x1, waiting for transfers between devices, on_device(): lax.psum_scatter(in_weight_part.astype(jnp.bfloat16), 'fsdp', scatter_dim...  34.3 us
    unnamed x2, blocking collectives  33.7 us
    while x108, local copies, waits for them, and re-layouts  30.4 us
    all_gather x1, waiting for transfers between devices, on_device(): lax.all_gather(in_weight, 'fsdp', axis=0, tiled=True)  22.8 us
    all_gather x1, blocking collectives, on_device(): all_pos = lax.all_gather(query_pos, 'ctx', axis=0, tiled=True)  22.5 us
    dot_general x4, matrix products, softmax_step(): jnp.einsum('qhd,khd->hqk', queries, keys, preferred_element_type=jnp.floa...  22.1 us
  transfers between devices with their start and end apart: 49, of which 42 were waited for; matrix products, arithmetic and copies ran while one was open for 38% of the time, Pallas kernels for 0%

profile of v1, /device:TPU:0, one launch (start us, length us, event | category | flops | bytes accessed | tf_op | source)
XLA Modules:
  0.0 682.0 jit_solution(3325261085705835145)
XLA Ops:
  14.8 18.4 %all-reduce.17 = (bf16[768]{0:T(1024)(128)(2,1)}, bf16[768]{0:T(1024)(128)(2,1)}, bf16[2304]{0:T(1024)(128)(2,1)S(1)}, bf16[768]{0:T(1024)(128)(2,1)S(1)}, bf16[768]{0:T(1024)(128)(2,1)S(1)}) all-reduce(bf16[768]{0:T(1024)(128)(2,1)S(1)} %dynamic-update-slice.5, ...), channel_id=1, replica_groups=mesh['fsdp'=4,'ctx'=8] {'fsdp'}, use_global_device_ids=true, to_apply=%add.5 | all-reduce | flops 5376 | bytes 21504
  37.1 22.8 %all-gather.8.cloned.1.call-done = bf16[768,2304]{1,0:T(8,128)(2,1)} async-done(((bf16[192,2304]{1,0:T(8,128)(2,1)}), bf16[768,2304]{1,0:T(8,128)(2,1)}) %all-gather.8.cloned.1.call-update) | async-done | bytes 3538960 | tf_op jit(solution)/shard_map/all_gather | solution.py:125
  60.0 4.7 convolution_add_fusion
  73.3 3.5 collective-permute-start.5
  76.8 11.5 %collective-permute-done.4 = bf16[256,12,64]{0,2,1:T(8,128)(2,1)S(1)} collective-permute-done((bf16[256,12,64]{0,2,1:T(8,128)(2,1)}, bf16[256,12,64]{0,2,1:T(8,128)(2,1)S(1)}, u32[]{:S(2)}, u32[]{:S(2)}) %collective-permute-start.4) | collective-permute-done | bytes 393248 | tf_op jit(solution)/shard_map/ppermute | solution.py:19
  88.4 5.0 collective-permute-done.5
  93.4 3.7 collective-permute-start.7
  97.2 6.7 collective-permute-done.6
  108.1 8.3 %all-gather.1 = bf16[4,1,768]{2,1,0:T(2,128)(2,1)S(1)} all-gather(bf16[1,1,768]{2,1,0:T(2,128)(2,1)S(1)} %reshape.292), channel_id=1, replica_groups=mesh['fsdp'=4,'ctx'=8] {'fsdp'}, dimensions={0}, use_global_device_ids=true | all-gather | bytes 7680 | tf_op jit(solution)/shard_map/all_gather | solution.py:130
  117.0 22.5 %all-gather = s32[1,2048]{1,0:T(1,128)} all-gather(s32[1,256]{1,0:T(1,128)} %param.20), channel_id=2, replica_groups=mesh['fsdp'=4,'ctx'=8] {'ctx'}, dimensions={1}, use_global_device_ids=true | all-gather | bytes 9216 | tf_op jit(solution)/shard_map/all_gather | solution.py:157
  156.7 63.9 %while.39 = (s32[]{:T(128)}, f32[12,256]{1,0:T(8,128)S(1)}, f32[12,256]{1,0:T(8,128)S(1)}, f32[256,12,64]{0,2,1:T(8,128)S(1)}, s32[4]{0:T(128)S(1)}, /*index=5*/...) while((s32[]{:T(128)}, f32[12,256]{1,0:T(8,128)S(1)}, ...), condition=%wide.region_5.6_spmd.clone, body=%wide.region_2.5_spmd.clone.sunk | while | flops 420694016 | bytes 48307420 | solution.py:199
  160.9 5.5 fusion.175
  166.4 4.8 fusion.179
  176.7 5.5 fusion.175
  182.3 4.8 fusion.179
  192.6 5.6 fusion.175
  198.2 4.8 fusion.179
  208.5 5.4 fusion.175
  214.0 5.2 fusion.179
  222.7 11.4 %multiply_convert_fusion.1 = (bf16[256,3072]{1,0:T(8,128)(2,1)S(1)}, f32[256,3072]{1,0:T(8,128)}, f32[256,3072]{1,0:T(8,128)}) fusion(f32[3072]{0:T(1024)S(1)} %bitcast.231, bf16[768,3072]{1,0:T(8,128)(2,1)} %all-gather.14.cloned.1.call-done, bf16[1,256,768]{2,1,0:T(8,128)(2,1)S(1)} %copy-done.3, f32[768]{0:T(1024)S(1)} %copy-done.32, ...), kind=kOutput, calls=%fused_computation.54 | convolution fusion | flops 1261043712 | bytes 12996608 | tf_op jit(solution)/shard_map/dot_general | solution.py:204
  234.1 7.8 %all-gather.16.cloned.1.call-done = bf16[3072,768]{1,0:T(8,128)(2,1)} async-done(((bf16[768,768]{1,0:T(8,128)(2,1)}), bf16[3072,768]{1,0:T(8,128)(2,1)}) %all-gather.16.cloned.1.call-update) | async-done | bytes 4718608 | tf_op jit(solution)/shard_map/all_gather | solution.py:131
  242.0 6.8 %fusion.121 = (bf16[3072]{0:T(1024)(128)(2,1)}, bf16[256,3072]{1,0:T(8,128)(2,1)S(1)}) fusion(f32[256,3072]{1,0:T(8,128)} %get-tuple-element.563, f32[256,3072]{1,0:T(8,128)} %get-tuple-element.587, bf16[3072,768]{1,0:T(8,128)(2,1)} %all-gather.16.cloned.1.call-done, bf16[1,256,768]{2,1,0:T(8,128)(2,1)S(1)} %copy-done.4), kind=kOutput, calls=%fused_computation.181 | convolution fusion | flops 1219752960 | bytes 12982272 | tf_op jit(solution)/shard_map/dot_general | solution.py:63
  249.9 3.7 convolution_convert_fusion.1
  253.8 17.6 %all-gather.12.cloned.1.call-done = bf16[768,768]{1,0:T(8,128)(2,1)} async-done(((bf16[192,768]{1,0:T(8,128)(2,1)}), bf16[768,768]{1,0:T(8,128)(2,1)}) %all-gather.12.cloned.1.call-update) | async-done | bytes 1179664 | tf_op jit(solution)/shard_map/all_gather | solution.py:127
  275.8 3.5 convolution_convert_fusion
  283.0 244.8 %while.40 = (s32[]{:T(128)}, bf16[256,12,64]{0,2,1:T(8,128)(2,1)}, bf16[256,12,64]{0,2,1:T(8,128)(2,1)}, f32[256,12,64]{0,2,1:T(8,128)S(1)}, f32[256,12,64]{0,2,...) while((s32[]{:T(128)}, bf16[256,12,64]{0,2,1:T(8,128)(2,1)}, ...), condition=%wide.region_9.10_spmd.clone, body=%wide.region_8.9_spmd.clone.sunk | while | flops 513605632 | bytes 40837772 | solution.py:256
  291.6 2.6 fusion.192
  302.0 3.1 collective-permute-done.3
  309.3 4.2 collective-permute-done.1
  322.2 2.7 fusion.192
  327.8 3.6 collective-permute-done.2
  332.6 3.1 collective-permute-done.3
  339.9 4.2 collective-permute-done.1
  352.8 2.6 fusion.192
  357.0 5.1 collective-permute-done.2
  363.1 3.1 collective-permute-done.3
  370.5 4.2 collective-permute-done.1
  387.7 5.0 collective-permute-done.2
  393.8 3.1 collective-permute-done.3
  401.2 4.2 collective-permute-done.1
  414.1 2.6 fusion.192
  418.4 5.1 collective-permute-done.2
  424.5 3.1 collective-permute-done.3
  431.8 4.2 collective-permute-done.1
  444.7 2.6 fusion.192
  448.9 5.1 collective-permute-done.2
  455.1 3.1 collective-permute-done.3
  462.4 4.2 collective-permute-done.1
  475.3 2.6 fusion.192
  479.5 5.1 collective-permute-done.2
  485.6 3.1 collective-permute-done.3
  493.0 4.2 collective-permute-done.1
  505.8 2.6 fusion.192
  510.1 5.1 collective-permute-done.2
  516.2 3.1 collective-permute-done.3
  523.6 4.2 collective-permute-done.1
  531.6 3.2 convolution_convert_fusion.2
  538.3 4.5 fusion.123
  545.1 34.3 %reduce-scatter.5.cloned.1.call-done = bf16[192,2304]{1,0:T(8,128)(2,1)} async-done(((bf16[768,2304]{1,0:T(8,128)(2,1)}), bf16[192,2304]{1,0:T(8,128)(2,1)}) %reduce-scatter.5.cloned.1.call-update) | async-done | bytes 884752 | tf_op jit(solution)/shard_map/reduce_scatter | solution.py:273
  581.3 15.4 %all-reduce.16 = (bf16[768]{0:T(1024)(128)(2,1)S(1)}, bf16[768]{0:T(1024)(128)(2,1)S(1)}, bf16[2304]{0:T(1024)(128)(2,1)S(1)}, bf16[768]{0:T(1024)(128)(2,1)S(1)...) all-reduce(bf16[768]{0:T(1024)(128)(2,1)S(1)} %dynamic-update-slice, ...), channel_id=1, replica_groups=mesh['fsdp'=4,'ctx'=8] {'fsdp'}, use_global_device_ids=true, to_apply=%add.6 | all-reduce | flops 10752 | bytes 43008
  597.2 15.3 %all-reduce.14 = (bf16[576]{0:T(1024)(128)(2,1)S(1)}, bf16[192]{0:T(256)(128)(2,1)S(1)}, bf16[768]{0:T(1024)(128)(2,1)S(1)}, bf16[192]{0:T(256)(128)(2,1)S(1)}, ...) all-reduce(bf16[576]{0:T(1024)(128)(2,1)S(1)} %dynamic-slice.8, ...), channel_id=1, replica_groups=mesh['fsdp'=4,'ctx'=8] {'ctx'}, use_global_device_ids=true, to_apply=%region_16.17 | all-reduce | flops 2304 | bytes 9216 | tf_op jit(solution)/shard_map/psum | solution.py:309
  616.0 3.9 convolution_add_fusion.3
  622.6 45.1 %all-reduce.20.cloned.1.call-done = (bf16[192,2304]{1,0:T(8,128)(2,1)}, bf16[192,768]{1,0:T(8,128)(2,1)}, bf16[192,3072]{1,0:T(8,128)(2,1)}, bf16[768,768]{1,0:T(8,128)(2,1)}) async-done(((bf16[192,2304]{1,0:T(8,128)(2,1)}, bf16[192,768]{1,0:T(8,128)(2,1)}, bf16[192,3072]{1,0:T(8,128)(2,1)}, bf16[768,768]{1,0:T(8,128)(2,1)}), (bf16[192,2304]{1,0:T(8,128)(2,1)}, bf16[192,768]{1,0:T(8,128)(2,1)}, ...) | async-done | bytes 3538960 | tf_op jit(solution)/shard_map/psum | solution.py:308
  667.7 3.1 convert_element_type.271
  (460 shorter events, 219.2 us)
Async XLA Ops:
  7.2 52.8 %all-gather.8.cloned.1.call-start = ((), (), s32[]{:S(2)}) async-start(), calls=%async_computation.4 | async-start | bytes 4423680 | tf_op jit(solution)/shard_map/all_gather | solution.py:125
  7.9 148.8 %all-gather.10.cloned.1.call-start = ((), (), s32[]{:S(2)}) async-start(), calls=%async_computation.5 | async-start | bytes 3538944 | tf_op jit(solution)/shard_map/all_gather | solution.py:187
  33.2 26.7 %copy-start.24 = (f32[768]{0:T(1024)}, f32[768]{0:T(1024)S(1)}, u32[]{:S(2)}) copy-start(f32[768]{0:T(1024)S(1)} %convert_element_type.241) | copy-start | bytes 9220
  33.2 26.7 %copy-start.30 = (f32[768]{0:T(1024)}, f32[768]{0:T(1024)S(1)}, u32[]{:S(2)}) copy-start(f32[768]{0:T(1024)S(1)} %convert_element_type.242) | copy-start | bytes 9220
  34.7 32.3 %copy-start.28 = (f32[256,16]{0,1:T(8,128)}, f32[256,16]{0,1:T(8,128)S(1)}, u32[]{:S(2)}) copy-start(f32[256,16]{0,1:T(8,128)S(1)} %get-tuple-element.584) | copy-start | bytes 49156
  35.8 24.1 %copy-start.34 = (f32[256]{0:T(256)}, f32[256]{0:T(256)S(1)}, u32[]{:S(2)}) copy-start(f32[256]{0:T(256)S(1)} %broadcast_multiply_fusion.1) | copy-start | bytes 3076
  37.1 22.9 %copy-start.43 = (f32[256]{0:T(256)}, f32[256]{0:T(256)S(1)}, u32[]{:S(2)}) copy-start(f32[256]{0:T(256)S(1)} %fusion.73) | copy-start | bytes 3076
  37.1 22.9 %copy-start.37 = (f32[256]{0:T(256)}, f32[256]{0:T(256)S(1)}, u32[]{:S(2)}) copy-start(f32[256]{0:T(256)S(1)} %fusion.109) | copy-start | bytes 3076
  69.0 153.7 %all-gather.14.cloned.1.call-start = ((), (), s32[]{:S(2)}) async-start(), calls=%async_computation.7 | async-start | bytes 5898240 | tf_op jit(solution)/shard_map/all_gather | solution.py:129
  69.7 172.3 %all-gather.16.cloned.1.call-start = ((), (), s32[]{:S(2)}) async-start(), calls=%async_computation.8 | async-start | bytes 5898240 | tf_op jit(solution)/shard_map/all_gather | solution.py:131
  70.3 201.1 %all-gather.12.cloned.1.call-start = ((), (), s32[]{:S(2)}) async-start(), calls=%async_computation.6 | async-start | bytes 1474560 | tf_op jit(solution)/shard_map/all_gather | solution.py:127
  73.3 15.1 %collective-permute-start.4 = (bf16[256,12,64]{0,2,1:T(8,128)(2,1)}, bf16[256,12,64]{0,2,1:T(8,128)(2,1)S(1)}, u32[]{:S(2)}, u32[]{:S(2)}) collective-permute-start(bf16[256,12,64]{0,2,1:T(8,128)(2,1)} %get-tuple-element.782), channel_id=1, source_target_pairs={{0,1},{1,2},{2,3},{3,4},{4,5},{5,6},{6,7},{7,0},{8,9},{9,10},{10,1... | collective-permute-start | bytes 1179656 | tf_op jit(solution)/shard_map/ppermute | solution.py:19
  73.3 20.1 %collective-permute-start.5 = (bf16[256,12,64]{0,2,1:T(8,128)(2,1)}, bf16[256,12,64]{0,2,1:T(8,128)(2,1)}, u32[]{:S(2)}, u32[]{:S(2)}) collective-permute-start(bf16[256,12,64]{0,2,1:T(8,128)(2,1)} %get-tuple-element.782), channel_id=1, source_target_pairs={{0,7},{1,0},{2,1},{3,2},{4,3},{5,4},{6,5},{7,6},{8,15},{9,8},{10,9... | collective-permute-start | bytes 1179656 | tf_op jit(solution)/shard_map/ppermute | solution.py:22
  88.4 51.2 %copy-start.22 = (bf16[256,12,64]{0,2,1:T(8,128)(2,1)}, bf16[256,12,64]{0,2,1:T(8,128)(2,1)S(1)}, u32[]{:S(2)}) copy-start(bf16[256,12,64]{0,2,1:T(8,128)(2,1)S(1)} %collective-permute-done.4) | copy-start | bytes 1179652
  88.4 15.5 %collective-permute-start.6 = (bf16[256,12,64]{0,2,1:T(8,128)(2,1)S(1)}, bf16[256,12,64]{0,2,1:T(8,128)(2,1)S(1)}, u32[]{:S(2)}, u32[]{:S(2)}) collective-permute-start(bf16[256,12,64]{0,2,1:T(8,128)(2,1)S(1)} %collective-permute-done.4), channel_id=1, source_target_pairs={{0,1},{1,2},{2,3},{3,4},{4,5},{5,6},{6,7},{7,0},{8,9},{9,10},{10,1... | collective-permute-start | bytes 1179656 | tf_op jit(solution)/shard_map/ppermute | solution.py:19
  93.4 48.9 %collective-permute-start.7 = (bf16[256,12,64]{0,2,1:T(8,128)(2,1)}, bf16[256,12,64]{0,2,1:T(8,128)(2,1)S(1)}, u32[]{:S(2)}, u32[]{:S(2)}) collective-permute-start(bf16[256,12,64]{0,2,1:T(8,128)(2,1)} %collective-permute-done.5), channel_id=1, source_target_pairs={{0,7},{1,0},{2,1},{3,2},{4,3},{5,4},{6,5},{7,6},{8,15},{9,8},{10,9... | collective-permute-start | bytes 1179656 | tf_op jit(solution)/shard_map/ppermute | solution.py:22
  97.1 447.9 %reduce-scatter.7.cloned.1.call-start = ((), (), s32[]{:S(2)}) async-start(), calls=%async_computation.10 | async-start | bytes 1474560 | tf_op jit(solution)/shard_map/reduce_scatter | solution.py:279
  103.9 42.7 %collective-permute-start.8 = (bf16[256,12,64]{0,2,1:T(8,128)(2,1)S(1)}, bf16[256,12,64]{0,2,1:T(8,128)(2,1)}, u32[]{:S(2)}, u32[]{:S(2)}) collective-permute-start(bf16[256,12,64]{0,2,1:T(8,128)(2,1)S(1)} %collective-permute-done.6), channel_id=1, source_target_pairs={{0,1},{1,2},{2,3},{3,4},{4,5},{5,6},{6,7},{7,0},{8,9},{9,10},{10,1... | collective-permute-start | bytes 1179656 | tf_op jit(solution)/shard_map/ppermute | solution.py:19
  139.6 17.2 %copy-start.50 = (s32[4]{0:T(128)S(1)}, s32[4]{0:T(128)}, u32[]{:S(2)}) copy-start(s32[4]{0:T(128)} %iota_multiply_fusion) | copy-start | bytes 52
  142.3 10.3 %collective-permute-start.9 = (bf16[256,12,64]{0,2,1:T(8,128)(2,1)S(1)}, bf16[256,12,64]{0,2,1:T(8,128)(2,1)S(1)}, u32[]{:S(2)}, u32[]{:S(2)}) collective-permute-start(bf16[256,12,64]{0,2,1:T(8,128)(2,1)S(1)} %collective-permute-done.7), channel_id=1, source_target_pairs={{0,7},{1,0},{2,1},{3,2},{4,3},{5,4},{6,5},{7,6},{8,15},{9,8},{10,9... | collective-permute-start | bytes 1179656 | tf_op jit(solution)/shard_map/ppermute | solution.py:22
  146.6 9.3 %collective-permute-start.10 = (bf16[256,12,64]{0,2,1:T(8,128)(2,1)}, bf16[256,12,64]{0,2,1:T(8,128)(2,1)S(1)}, u32[]{:S(2)}, u32[]{:S(2)}) collective-permute-start(bf16[256,12,64]{0,2,1:T(8,128)(2,1)} %collective-permute-done.8), channel_id=1, source_target_pairs={{0,1},{1,2},{2,3},{3,4},{4,5},{5,6},{6,7},{7,0},{8,9},{9,10},{10,1... | collective-permute-start | bytes 1179656 | tf_op jit(solution)/shard_map/ppermute | solution.py:19
  156.7 64.1 %copy-start.4 = (bf16[1,256,768]{2,1,0:T(8,128)(2,1)S(1)}, bf16[1,256,768]{2,1,0:T(8,128)(2,1)}, u32[]{:S(2)}) copy-start(bf16[1,256,768]{2,1,0:T(8,128)(2,1)} %param.33) | copy-start | bytes 1179652
  220.7 13.4 %copy-start.17 = (f32[12,256]{1,0:T(8,128)}, f32[12,256]{1,0:T(8,128)S(1)}, u32[]{:S(2)}) copy-start(f32[12,256]{1,0:T(8,128)S(1)} %get-tuple-element.380) | copy-start | bytes 36868
  222.4 322.6 %reduce-scatter.9.cloned.1.call-start = ((), (), s32[]{:S(2)}) async-start(), calls=%async_computation.11 | async-start | bytes 5898240 | tf_op jit(solution)/shard_map/reduce_scatter | solution.py:285
  234.1 41.7 %copy-start.9 = (bf16[256,3072]{1,0:T(8,128)(2,1)}, bf16[256,3072]{1,0:T(8,128)(2,1)S(1)}, u32[]{:S(2)}) copy-start(bf16[256,3072]{1,0:T(8,128)(2,1)S(1)} %get-tuple-element.562) | copy-start | bytes 4718596
  253.7 291.4 %reduce-scatter.11.cloned.1.call-start = ((), (), s32[]{:S(2)}) async-start(), calls=%async_computation.12 | async-start | bytes 5898240 | tf_op jit(solution)/shard_map/reduce_scatter | solution.py:291
  279.4 299.9 %reduce-scatter.5.cloned.1.call-start = ((), (), s32[]{:S(2)}) async-start(), calls=%async_computation.9 | async-start | bytes 4423680 | tf_op jit(solution)/shard_map/reduce_scatter | solution.py:273
  283.0 247.1 %copy-start.29 = (f32[256,16]{0,1:T(8,128)S(1)}, f32[256,16]{0,1:T(8,128)}, u32[]{:S(2)}) copy-start(f32[256,16]{0,1:T(8,128)} %copy-done.28) | copy-start | bytes 49156
  291.6 9.3 %collective-permute-start.2 = (bf16[256,12,64]{0,2,1:T(8,128)(2,1)}, bf16[256,12,64]{0,2,1:T(8,128)(2,1)}, u32[]{:S(2)}, u32[]{:S(2)}) collective-permute-start(bf16[256,12,64]{0,2,1:T(8,128)(2,1)} %fusion.191), channel_id=1, source_target_pairs={{0,1},{1,2},{2,3},{3,4},{4,5},{5,6},{6,7},{7,0},{8,9},{9,10},{10,1... | collective-permute-start | bytes 1179656 | tf_op jit(solution)/shard_map/while/body/eval_jaxpr/ppermute | solution.py:31
  294.2 10.9 %collective-permute-start.3 = (bf16[256,12,64]{0,2,1:T(8,128)(2,1)}, bf16[256,12,64]{0,2,1:T(8,128)(2,1)}, u32[]{:S(2)}, u32[]{:S(2)}) collective-permute-start(bf16[256,12,64]{0,2,1:T(8,128)(2,1)} %fusion.192), channel_id=1, source_target_pairs={{0,1},{1,2},{2,3},{3,4},{4,5},{5,6},{6,7},{7,0},{8,9},{9,10},{10,1... | collective-permute-start | bytes 1179656 | tf_op jit(solution)/shard_map/while/body/eval_jaxpr/ppermute | solution.py:31
  295.7 13.7 %collective-permute-start = (bf16[256,12,64]{0,2,1:T(8,128)(2,1)S(1)}, bf16[256,12,64]{0,2,1:T(8,128)(2,1)}, u32[]{:S(2)}, u32[]{:S(2)}) collective-permute-start(bf16[256,12,64]{0,2,1:T(8,128)(2,1)S(1)} %copy.84), channel_id=1, source_target_pairs={{0,1},{1,2},{2,3},{3,4},{4,5},{5,6},{6,7},{7,0},{8,9},{9,10},{10,1... | collective-permute-start | bytes 1179656 | tf_op jit(solution)/shard_map/while/body/eval_jaxpr/ppermute | solution.py:31
  295.8 17.8 %collective-permute-start.1 = (bf16[256,12,64]{0,2,1:T(8,128)(2,1)}, bf16[256,12,64]{0,2,1:T(8,128)(2,1)}, u32[]{:S(2)}, u32[]{:S(2)}) collective-permute-start(bf16[256,12,64]{0,2,1:T(8,128)(2,1)} %copy.85), channel_id=1, source_target_pairs={{0,1},{1,2},{2,3},{3,4},{4,5},{5,6},{6,7},{7,0},{8,9},{9,10},{10,1... | collective-permute-start | bytes 1179656 | tf_op jit(solution)/shard_map/while/body/eval_jaxpr/ppermute | solution.py:31
  322.2 9.3 %collective-permute-start.2 = (bf16[256,12,64]{0,2,1:T(8,128)(2,1)}, bf16[256,12,64]{0,2,1:T(8,128)(2,1)}, u32[]{:S(2)}, u32[]{:S(2)}) collective-permute-start(bf16[256,12,64]{0,2,1:T(8,128)(2,1)} %fusion.191), channel_id=1, source_target_pairs={{0,1},{1,2},{2,3},{3,4},{4,5},{5,6},{6,7},{7,0},{8,9},{9,10},{10,1... | collective-permute-start | bytes 1179656 | tf_op jit(solution)/shard_map/while/body/eval_jaxpr/ppermute | solution.py:31
  324.9 10.8 %collective-permute-start.3 = (bf16[256,12,64]{0,2,1:T(8,128)(2,1)}, bf16[256,12,64]{0,2,1:T(8,128)(2,1)}, u32[]{:S(2)}, u32[]{:S(2)}) collective-permute-start(bf16[256,12,64]{0,2,1:T(8,128)(2,1)} %fusion.192), channel_id=1, source_target_pairs={{0,1},{1,2},{2,3},{3,4},{4,5},{5,6},{6,7},{7,0},{8,9},{9,10},{10,1... | collective-permute-start | bytes 1179656 | tf_op jit(solution)/shard_map/while/body/eval_jaxpr/ppermute | solution.py:31
  324.9 15.1 %collective-permute-start = (bf16[256,12,64]{0,2,1:T(8,128)(2,1)S(1)}, bf16[256,12,64]{0,2,1:T(8,128)(2,1)}, u32[]{:S(2)}, u32[]{:S(2)}) collective-permute-start(bf16[256,12,64]{0,2,1:T(8,128)(2,1)S(1)} %copy.84), channel_id=1, source_target_pairs={{0,1},{1,2},{2,3},{3,4},{4,5},{5,6},{6,7},{7,0},{8,9},{9,10},{10,1... | collective-permute-start | bytes 1179656 | tf_op jit(solution)/shard_map/while/body/eval_jaxpr/ppermute | solution.py:31
  324.9 19.3 %collective-permute-start.1 = (bf16[256,12,64]{0,2,1:T(8,128)(2,1)}, bf16[256,12,64]{0,2,1:T(8,128)(2,1)}, u32[]{:S(2)}, u32[]{:S(2)}) collective-permute-start(bf16[256,12,64]{0,2,1:T(8,128)(2,1)} %copy.85), channel_id=1, source_target_pairs={{0,1},{1,2},{2,3},{3,4},{4,5},{5,6},{6,7},{7,0},{8,9},{9,10},{10,1... | collective-permute-start | bytes 1179656 | tf_op jit(solution)/shard_map/while/body/eval_jaxpr/ppermute | solution.py:31
  352.8 9.3 %collective-permute-start.2 = (bf16[256,12,64]{0,2,1:T(8,128)(2,1)}, bf16[256,12,64]{0,2,1:T(8,128)(2,1)}, u32[]{:S(2)}, u32[]{:S(2)}) collective-permute-start(bf16[256,12,64]{0,2,1:T(8,128)(2,1)} %fusion.191), channel_id=1, source_target_pairs={{0,1},{1,2},{2,3},{3,4},{4,5},{5,6},{6,7},{7,0},{8,9},{9,10},{10,1... | collective-permute-start | bytes 1179656 | tf_op jit(solution)/shard_map/while/body/eval_jaxpr/ppermute | solution.py:31
  355.4 10.9 %collective-permute-start.3 = (bf16[256,12,64]{0,2,1:T(8,128)(2,1)}, bf16[256,12,64]{0,2,1:T(8,128)(2,1)}, u32[]{:S(2)}, u32[]{:S(2)}) collective-permute-start(bf16[256,12,64]{0,2,1:T(8,128)(2,1)} %fusion.192), channel_id=1, source_target_pairs={{0,1},{1,2},{2,3},{3,4},{4,5},{5,6},{6,7},{7,0},{8,9},{9,10},{10,1... | collective-permute-start | bytes 1179656 | tf_op jit(solution)/shard_map/while/body/eval_jaxpr/ppermute | solution.py:31
  355.4 15.1 %collective-permute-start = (bf16[256,12,64]{0,2,1:T(8,128)(2,1)S(1)}, bf16[256,12,64]{0,2,1:T(8,128)(2,1)}, u32[]{:S(2)}, u32[]{:S(2)}) collective-permute-start(bf16[256,12,64]{0,2,1:T(8,128)(2,1)S(1)} %copy.84), channel_id=1, source_target_pairs={{0,1},{1,2},{2,3},{3,4},{4,5},{5,6},{6,7},{7,0},{8,9},{9,10},{10,1... | collective-permute-start | bytes 1179656 | tf_op jit(solution)/shard_map/while/body/eval_jaxpr/ppermute | solution.py:31
  355.4 19.3 %collective-permute-start.1 = (bf16[256,12,64]{0,2,1:T(8,128)(2,1)}, bf16[256,12,64]{0,2,1:T(8,128)(2,1)}, u32[]{:S(2)}, u32[]{:S(2)}) collective-permute-start(bf16[256,12,64]{0,2,1:T(8,128)(2,1)} %copy.85), channel_id=1, source_target_pairs={{0,1},{1,2},{2,3},{3,4},{4,5},{5,6},{6,7},{7,0},{8,9},{9,10},{10,1... | collective-permute-start | bytes 1179656 | tf_op jit(solution)/shard_map/while/body/eval_jaxpr/ppermute | solution.py:31
  383.4 9.3 %collective-permute-start.2 = (bf16[256,12,64]{0,2,1:T(8,128)(2,1)}, bf16[256,12,64]{0,2,1:T(8,128)(2,1)}, u32[]{:S(2)}, u32[]{:S(2)}) collective-permute-start(bf16[256,12,64]{0,2,1:T(8,128)(2,1)} %fusion.191), channel_id=1, source_target_pairs={{0,1},{1,2},{2,3},{3,4},{4,5},{5,6},{6,7},{7,0},{8,9},{9,10},{10,1... | collective-permute-start | bytes 1179656 | tf_op jit(solution)/shard_map/while/body/eval_jaxpr/ppermute | solution.py:31
  386.1 10.8 %collective-permute-start.3 = (bf16[256,12,64]{0,2,1:T(8,128)(2,1)}, bf16[256,12,64]{0,2,1:T(8,128)(2,1)}, u32[]{:S(2)}, u32[]{:S(2)}) collective-permute-start(bf16[256,12,64]{0,2,1:T(8,128)(2,1)} %fusion.192), channel_id=1, source_target_pairs={{0,1},{1,2},{2,3},{3,4},{4,5},{5,6},{6,7},{7,0},{8,9},{9,10},{10,1... | collective-permute-start | bytes 1179656 | tf_op jit(solution)/shard_map/while/body/eval_jaxpr/ppermute | solution.py:31
  386.1 15.1 %collective-permute-start = (bf16[256,12,64]{0,2,1:T(8,128)(2,1)S(1)}, bf16[256,12,64]{0,2,1:T(8,128)(2,1)}, u32[]{:S(2)}, u32[]{:S(2)}) collective-permute-start(bf16[256,12,64]{0,2,1:T(8,128)(2,1)S(1)} %copy.84), channel_id=1, source_target_pairs={{0,1},{1,2},{2,3},{3,4},{4,5},{5,6},{6,7},{7,0},{8,9},{9,10},{10,1... | collective-permute-start | bytes 1179656 | tf_op jit(solution)/shard_map/while/body/eval_jaxpr/ppermute | solution.py:31
  386.1 19.3 %collective-permute-start.1 = (bf16[256,12,64]{0,2,1:T(8,128)(2,1)}, bf16[256,12,64]{0,2,1:T(8,128)(2,1)}, u32[]{:S(2)}, u32[]{:S(2)}) collective-permute-start(bf16[256,12,64]{0,2,1:T(8,128)(2,1)} %copy.85), channel_id=1, source_target_pairs={{0,1},{1,2},{2,3},{3,4},{4,5},{5,6},{6,7},{7,0},{8,9},{9,10},{10,1... | collective-permute-start | bytes 1179656 | tf_op jit(solution)/shard_map/while/body/eval_jaxpr/ppermute | solution.py:31
  414.1 9.3 %collective-permute-start.2 = (bf16[256,12,64]{0,2,1:T(8,128)(2,1)}, bf16[256,12,64]{0,2,1:T(8,128)(2,1)}, u32[]{:S(2)}, u32[]{:S(2)}) collective-permute-start(bf16[256,12,64]{0,2,1:T(8,128)(2,1)} %fusion.191), channel_id=1, source_target_pairs={{0,1},{1,2},{2,3},{3,4},{4,5},{5,6},{6,7},{7,0},{8,9},{9,10},{10,1... | collective-permute-start | bytes 1179656 | tf_op jit(solution)/shard_map/while/body/eval_jaxpr/ppermute | solution.py:31
  416.7 10.9 %collective-permute-start.3 = (bf16[256,12,64]{0,2,1:T(8,128)(2,1)}, bf16[256,12,64]{0,2,1:T(8,128)(2,1)}, u32[]{:S(2)}, u32[]{:S(2)}) collective-permute-start(bf16[256,12,64]{0,2,1:T(8,128)(2,1)} %fusion.192), channel_id=1, source_target_pairs={{0,1},{1,2},{2,3},{3,4},{4,5},{5,6},{6,7},{7,0},{8,9},{9,10},{10,1... | collective-permute-start | bytes 1179656 | tf_op jit(solution)/shard_map/while/body/eval_jaxpr/ppermute | solution.py:31
  416.7 15.1 %collective-permute-start = (bf16[256,12,64]{0,2,1:T(8,128)(2,1)S(1)}, bf16[256,12,64]{0,2,1:T(8,128)(2,1)}, u32[]{:S(2)}, u32[]{:S(2)}) collective-permute-start(bf16[256,12,64]{0,2,1:T(8,128)(2,1)S(1)} %copy.84), channel_id=1, source_target_pairs={{0,1},{1,2},{2,3},{3,4},{4,5},{5,6},{6,7},{7,0},{8,9},{9,10},{10,1... | collective-permute-start | bytes 1179656 | tf_op jit(solution)/shard_map/while/body/eval_jaxpr/ppermute | solution.py:31
  416.7 19.3 %collective-permute-start.1 = (bf16[256,12,64]{0,2,1:T(8,128)(2,1)}, bf16[256,12,64]{0,2,1:T(8,128)(2,1)}, u32[]{:S(2)}, u32[]{:S(2)}) collective-permute-start(bf16[256,12,64]{0,2,1:T(8,128)(2,1)} %copy.85), channel_id=1, source_target_pairs={{0,1},{1,2},{2,3},{3,4},{4,5},{5,6},{6,7},{7,0},{8,9},{9,10},{10,1... | collective-permute-start | bytes 1179656 | tf_op jit(solution)/shard_map/while/body/eval_jaxpr/ppermute | solution.py:31
  444.7 9.3 %collective-permute-start.2 = (bf16[256,12,64]{0,2,1:T(8,128)(2,1)}, bf16[256,12,64]{0,2,1:T(8,128)(2,1)}, u32[]{:S(2)}, u32[]{:S(2)}) collective-permute-start(bf16[256,12,64]{0,2,1:T(8,128)(2,1)} %fusion.191), channel_id=1, source_target_pairs={{0,1},{1,2},{2,3},{3,4},{4,5},{5,6},{6,7},{7,0},{8,9},{9,10},{10,1... | collective-permute-start | bytes 1179656 | tf_op jit(solution)/shard_map/while/body/eval_jaxpr/ppermute | solution.py:31
  447.3 10.9 %collective-permute-start.3 = (bf16[256,12,64]{0,2,1:T(8,128)(2,1)}, bf16[256,12,64]{0,2,1:T(8,128)(2,1)}, u32[]{:S(2)}, u32[]{:S(2)}) collective-permute-start(bf16[256,12,64]{0,2,1:T(8,128)(2,1)} %fusion.192), channel_id=1, source_target_pairs={{0,1},{1,2},{2,3},{3,4},{4,5},{5,6},{6,7},{7,0},{8,9},{9,10},{10,1... | collective-permute-start | bytes 1179656 | tf_op jit(solution)/shard_map/while/body/eval_jaxpr/ppermute | solution.py:31
  447.3 15.1 %collective-permute-start = (bf16[256,12,64]{0,2,1:T(8,128)(2,1)S(1)}, bf16[256,12,64]{0,2,1:T(8,128)(2,1)}, u32[]{:S(2)}, u32[]{:S(2)}) collective-permute-start(bf16[256,12,64]{0,2,1:T(8,128)(2,1)S(1)} %copy.84), channel_id=1, source_target_pairs={{0,1},{1,2},{2,3},{3,4},{4,5},{5,6},{6,7},{7,0},{8,9},{9,10},{10,1... | collective-permute-start | bytes 1179656 | tf_op jit(solution)/shard_map/while/body/eval_jaxpr/ppermute | solution.py:31
  447.3 19.3 %collective-permute-start.1 = (bf16[256,12,64]{0,2,1:T(8,128)(2,1)}, bf16[256,12,64]{0,2,1:T(8,128)(2,1)}, u32[]{:S(2)}, u32[]{:S(2)}) collective-permute-start(bf16[256,12,64]{0,2,1:T(8,128)(2,1)} %copy.85), channel_id=1, source_target_pairs={{0,1},{1,2},{2,3},{3,4},{4,5},{5,6},{6,7},{7,0},{8,9},{9,10},{10,1... | collective-permute-start | bytes 1179656 | tf_op jit(solution)/shard_map/while/body/eval_jaxpr/ppermute | solution.py:31
  475.3 9.3 %collective-permute-start.2 = (bf16[256,12,64]{0,2,1:T(8,128)(2,1)}, bf16[256,12,64]{0,2,1:T(8,128)(2,1)}, u32[]{:S(2)}, u32[]{:S(2)}) collective-permute-start(bf16[256,12,64]{0,2,1:T(8,128)(2,1)} %fusion.191), channel_id=1, source_target_pairs={{0,1},{1,2},{2,3},{3,4},{4,5},{5,6},{6,7},{7,0},{8,9},{9,10},{10,1... | collective-permute-start | bytes 1179656 | tf_op jit(solution)/shard_map/while/body/eval_jaxpr/ppermute | solution.py:31
  477.9 10.9 %collective-permute-start.3 = (bf16[256,12,64]{0,2,1:T(8,128)(2,1)}, bf16[256,12,64]{0,2,1:T(8,128)(2,1)}, u32[]{:S(2)}, u32[]{:S(2)}) collective-permute-start(bf16[256,12,64]{0,2,1:T(8,128)(2,1)} %fusion.192), channel_id=1, source_target_pairs={{0,1},{1,2},{2,3},{3,4},{4,5},{5,6},{6,7},{7,0},{8,9},{9,10},{10,1... | collective-permute-start | bytes 1179656 | tf_op jit(solution)/shard_map/while/body/eval_jaxpr/ppermute | solution.py:31
  477.9 15.1 %collective-permute-start = (bf16[256,12,64]{0,2,1:T(8,128)(2,1)S(1)}, bf16[256,12,64]{0,2,1:T(8,128)(2,1)}, u32[]{:S(2)}, u32[]{:S(2)}) collective-permute-start(bf16[256,12,64]{0,2,1:T(8,128)(2,1)S(1)} %copy.84), channel_id=1, source_target_pairs={{0,1},{1,2},{2,3},{3,4},{4,5},{5,6},{6,7},{7,0},{8,9},{9,10},{10,1... | collective-permute-start | bytes 1179656 | tf_op jit(solution)/shard_map/while/body/eval_jaxpr/ppermute | solution.py:31
  477.9 19.3 %collective-permute-start.1 = (bf16[256,12,64]{0,2,1:T(8,128)(2,1)}, bf16[256,12,64]{0,2,1:T(8,128)(2,1)}, u32[]{:S(2)}, u32[]{:S(2)}) collective-permute-start(bf16[256,12,64]{0,2,1:T(8,128)(2,1)} %copy.85), channel_id=1, source_target_pairs={{0,1},{1,2},{2,3},{3,4},{4,5},{5,6},{6,7},{7,0},{8,9},{9,10},{10,1... | collective-permute-start | bytes 1179656 | tf_op jit(solution)/shard_map/while/body/eval_jaxpr/ppermute | solution.py:31
  505.8 9.3 %collective-permute-start.2 = (bf16[256,12,64]{0,2,1:T(8,128)(2,1)}, bf16[256,12,64]{0,2,1:T(8,128)(2,1)}, u32[]{:S(2)}, u32[]{:S(2)}) collective-permute-start(bf16[256,12,64]{0,2,1:T(8,128)(2,1)} %fusion.191), channel_id=1, source_target_pairs={{0,1},{1,2},{2,3},{3,4},{4,5},{5,6},{6,7},{7,0},{8,9},{9,10},{10,1... | collective-permute-start | bytes 1179656 | tf_op jit(solution)/shard_map/while/body/eval_jaxpr/ppermute | solution.py:31
  508.5 10.9 %collective-permute-start.3 = (bf16[256,12,64]{0,2,1:T(8,128)(2,1)}, bf16[256,12,64]{0,2,1:T(8,128)(2,1)}, u32[]{:S(2)}, u32[]{:S(2)}) collective-permute-start(bf16[256,12,64]{0,2,1:T(8,128)(2,1)} %fusion.192), channel_id=1, source_target_pairs={{0,1},{1,2},{2,3},{3,4},{4,5},{5,6},{6,7},{7,0},{8,9},{9,10},{10,1... | collective-permute-start | bytes 1179656 | tf_op jit(solution)/shard_map/while/body/eval_jaxpr/ppermute | solution.py:31
  508.5 15.1 %collective-permute-start = (bf16[256,12,64]{0,2,1:T(8,128)(2,1)S(1)}, bf16[256,12,64]{0,2,1:T(8,128)(2,1)}, u32[]{:S(2)}, u32[]{:S(2)}) collective-permute-start(bf16[256,12,64]{0,2,1:T(8,128)(2,1)S(1)} %copy.84), channel_id=1, source_target_pairs={{0,1},{1,2},{2,3},{3,4},{4,5},{5,6},{6,7},{7,0},{8,9},{9,10},{10,1... | collective-permute-start | bytes 1179656 | tf_op jit(solution)/shard_map/while/body/eval_jaxpr/ppermute | solution.py:31
  508.5 19.3 %collective-permute-start.1 = (bf16[256,12,64]{0,2,1:T(8,128)(2,1)}, bf16[256,12,64]{0,2,1:T(8,128)(2,1)}, u32[]{:S(2)}, u32[]{:S(2)}) collective-permute-start(bf16[256,12,64]{0,2,1:T(8,128)(2,1)} %copy.85), channel_id=1, source_target_pairs={{0,1},{1,2},{2,3},{3,4},{4,5},{5,6},{6,7},{7,0},{8,9},{9,10},{10,1... | collective-permute-start | bytes 1179656 | tf_op jit(solution)/shard_map/while/body/eval_jaxpr/ppermute | solution.py:31
  534.8 132.9 %all-reduce.20.cloned.1.call-start = ((), (), s32[]{:S(2)}) async-start(), calls=%async_computation.13 | async-start | bytes 7077888 | tf_op jit(solution)/shard_map/psum | solution.py:308
  545.0 36.3 %copy-start.45 = (bf16[3072]{0:T(1024)(128)(2,1)S(1)}, bf16[3072]{0:T(1024)(128)(2,1)}, u32[]{:S(2)}) copy-start(bf16[3072]{0:T(1024)(128)(2,1)} %get-tuple-element.588) | copy-start | bytes 18436
  545.0 71.0 %copy-start.10 = (bf16[256,3072]{1,0:T(8,128)(2,1)S(1)}, bf16[256,3072]{1,0:T(8,128)(2,1)}, u32[]{:S(2)}) copy-start(bf16[256,3072]{1,0:T(8,128)(2,1)} %copy-done.9) | copy-start | bytes 4718596
  613.7 60.9 %copy-start.46 = (f32[192]{0:T(256)}, f32[192]{0:T(256)S(1)}, u32[]{:S(2)}) copy-start(f32[192]{0:T(256)S(1)} %convert_element_type.269) | copy-start | bytes 2308
  (74 other events, 182.5 us)
Sparse Core Ops, SparseCore 0:
  9.9 50.0 all-gather.7
  69.1 57.2 all-gather.9
  128.3 54.8 all-gather.13
  184.8 57.0 all-gather.15
  243.6 27.7 all-gather.11
  274.7 28.5 reduce-scatter.6
  306.3 57.0 reduce-scatter.8
  366.4 57.0 reduce-scatter.10
  534.9 44.3 reduce-scatter.4
  581.8 85.8 all-reduce.19
